TPU v7x, 512 devices: a whole 4x8x8 slice. The times are simulated.
512 devices in a mesh: dp: 64 (over y_hi, z, x), tensor: 8 (over y_lo, core).
Axes of the slice: x: 4, y: 8 (y_hi: 2, y_lo: 4; y = y_hi * 4 + y_lo), z: 8, core: 2. Of those that a mesh axis runs over, the one named last changes fastest.
Arguments:
- acts: bfloat16 [2, 8192, 8192], P(None, ('dp', 'tensor')), may hold values from -6 to 6
- grad_out: bfloat16 [2, 8192, 8192], P(None, ('dp', 'tensor')), may hold values from -24 to 24
- w_gate: bfloat16 [8192, 128], P(None, 'tensor'), may hold values from -0.0625 to 0.0625
- w_up: bfloat16 [8192, 128], P(None, 'tensor'), may hold values from -0.0625 to 0.0625
- w_down: bfloat16 [128, 8192], P('tensor'), may hold values from -0.5 to 0.5
- overflow: int32 [64, 2], P('dp'), may hold values 0 or 1
- step: int32 [1], replicated, may hold values from 1 to 8
- master: float32 [3, 128, 8192], P(None, 'tensor', 'dp'), may hold values from -0.75 to 0.75
- moment1: float32 [3, 128, 8192], P(None, 'tensor', 'dp'), may hold values from -6 to 6
- moment2: float32 [3, 128, 8192], P(None, 'tensor', 'dp'), may hold values from 0.01 to 1
Outputs:
- new_master: float32 [3, 128, 8192], P(None, 'tensor', 'dp')
- new_moment1: float32 [3, 128, 8192], P(None, 'tensor', 'dp')
- new_moment2: float32 [3, 128, 8192], P(None, 'tensor', 'dp')
All inputs are finite; a program needn't handle non-finite values. No bound on the sum of `overflow` on one device may be relied on, other than what follows from the above.
Results may differ from a plain program's by a relative error of at most 0.0033.
Values may be sent and summed in bfloat16 or wider, within the bound.
A program may use at most 64 MiB of HBM per device.

v0:
```python
import jax
import jax.numpy as jnp
from jax import lax
from jax.sharding import PartitionSpec as P


def contract_rows(left, right):
    return lax.dot_general(
        left, right, (((0,), (0,)), ((), ())), preferred_element_type=jnp.float32
    )


def local_grads(rows_x, rows_dy, w_gate, w_up, w_down):
    gate = jnp.dot(rows_x, w_gate, preferred_element_type=jnp.float32)
    up = jnp.dot(rows_x, w_up, preferred_element_type=jnp.float32)
    sig = jax.nn.sigmoid(gate)
    silu = gate * sig
    hidden = (silu * up).astype(jnp.bfloat16)
    dh = lax.dot_general(
        rows_dy, w_down, (((1,), (1,)), ((), ())), preferred_element_type=jnp.float32
    )
    dup = (dh * silu).astype(jnp.bfloat16)
    dgate = (dh * up * sig * (1.0 + gate * (1.0 - sig))).astype(jnp.bfloat16)
    return jnp.stack(
        [contract_rows(dgate, rows_x), contract_rows(dup, rows_x), contract_rows(hidden, rows_dy)]
    )


def per_device(acts, grad_out, w_gate, w_up, w_down, overflow, step, master, moment1, moment2):
    n_dp = lax.axis_size("dp")
    micro = acts.shape[0]
    good = (1 - overflow[0]).astype(jnp.float32)
    total = jnp.zeros((3, w_down.shape[0], w_down.shape[1]), jnp.float32)
    for index in range(micro):
        rows_x, rows_dy = (
            lax.all_gather(acts[index], "tensor", axis=0, tiled=True),
            lax.all_gather(grad_out[index], "tensor", axis=0, tiled=True),
        )
        total = total + good[index] * local_grads(rows_x, rows_dy, w_gate, w_up, w_down)
    local_count = jnp.sum(overflow)
    count = lax.psum(local_count, "dp").astype(jnp.float32)
    summed = lax.psum_scatter(total, "dp", scatter_dimension=2, tiled=True)
    grad = summed / jnp.float32(micro * n_dp)
    keep = 1.0 - count / jnp.float32(micro * n_dp)
    new_moment1 = 0.9 * moment1 + 0.1 * grad
    new_moment2 = 0.95 * moment2 + 0.05 * grad * grad
    steps_f = step[0].astype(jnp.float32)
    corr1 = 1.0 - jnp.power(jnp.float32(0.9), steps_f)
    corr2 = 1.0 - jnp.power(jnp.float32(0.95), steps_f)
    direction = new_moment1 / corr1 / (jnp.sqrt(new_moment2 / corr2) + 1e-08)
    new_master = master - 0.01 * keep * (direction + 0.1 * master)
    return (new_master, new_moment1, new_moment2)


def solution(mesh):
    in_specs = (
        P(None, ("dp", "tensor"), None),
        P(None, ("dp", "tensor"), None),
        P(None, "tensor"),
        P(None, "tensor"),
        P("tensor", None),
        P("dp", None),
        P(),
        P(None, "tensor", "dp"),
        P(None, "tensor", "dp"),
        P(None, "tensor", "dp"),
    )
    out_specs = (P(None, "tensor", "dp"), P(None, "tensor", "dp"), P(None, "tensor", "dp"))
    return jax.shard_map(
        per_device, mesh=mesh, in_specs=in_specs, out_specs=out_specs, check_vma=False
    )
```

profile of v0, /device:TPU:1, one launch (start us, length us, event | category | flops | bytes accessed | tf_op | source)
XLA Modules:
  0.0 1022.7 jit_solution(17078261582251090015)
XLA Ops:
  7.2 0.0 copy-start
  7.2 0.0 copy-start.11
  7.2 0.0 all-gather.11.cloned.1.call-start
  7.2 1.9 fusion.33
  9.1 0.0 all-gather.11.cloned.1.call-update
  9.1 0.0 copy-start.6
  9.2 0.0 all-gather.9.cloned.1.call-start
  9.2 1.9 fusion.34
  11.1 0.0 all-gather.9.cloned.1.call-update
  11.2 0.0 all-gather.15.cloned.1.call-start
  11.2 0.7 all-gather.15.cloned.1.call-update
  11.9 0.0 all-gather.13.cloned.1.call-start
  11.9 0.5 all-gather.13.cloned.1.call-update
  12.5 0.0 reduce-scatter.2.cloned.1.call-start
  12.5 0.0 copy-done.11
  12.5 0.6 subtract_convert_fusion
  13.2 0.6 fusion.35
  13.7 42.2 %all-gather.11.cloned.1.call-done = bf16[1,128,8192]{2,1,0:T(8,128)(2,1)} async-done(((bf16[1,16,8192]{2,1,0:T(8,128)(2,1)}), bf16[1,128,8192]{2,1,0:T(8,128)(2,1)}) %all-gather.11.cloned.1.call-update) | async-done | bytes 2097168 | tf_op jit(solution)/shard_map/all_gather | solution.py:36
  56.0 0.0 copy-done
  56.0 0.0 copy-start.1
  56.0 2.4 fusion.13
  58.4 0.0 copy-done.6
  58.4 0.0 copy-done.1
  58.4 0.0 copy-start.7
  58.4 0.6 fusion.11
  59.0 40.5 %all-gather.9.cloned.1.call-done = bf16[1,128,8192]{2,1,0:T(8,128)(2,1)} async-done(((bf16[1,16,8192]{2,1,0:T(8,128)(2,1)}), bf16[1,128,8192]{2,1,0:T(8,128)(2,1)}) %all-gather.9.cloned.1.call-update) | async-done | bytes 2097168 | tf_op jit(solution)/shard_map/all_gather | solution.py:37
  99.5 0.0 copy-start.3
  99.5 2.1 convolution_bitcast_fusion.3
  101.6 0.0 copy-done.7
  101.6 0.1 copy-done.3
  101.7 0.6 fusion.16
  102.4 0.4 convolution_bitcast_fusion.4
  102.8 1.2 convolution_bitcast_fusion.5
  104.0 39.1 %all-gather.15.cloned.1.call-done = bf16[1,128,8192]{2,1,0:T(8,128)(2,1)} async-done(((bf16[1,16,8192]{2,1,0:T(8,128)(2,1)}), bf16[1,128,8192]{2,1,0:T(8,128)(2,1)}) %all-gather.15.cloned.1.call-update) | async-done | bytes 2097168 | tf_op jit(solution)/shard_map/all_gather | solution.py:36
  143.1 0.0 copy-start.2
  143.1 2.4 fusion.4
  145.5 0.0 copy-done.2
  145.5 1.6 fusion.2
  147.1 39.4 %all-gather.13.cloned.1.call-done = bf16[1,128,8192]{2,1,0:T(8,128)(2,1)} async-done(((bf16[1,16,8192]{2,1,0:T(8,128)(2,1)}), bf16[1,128,8192]{2,1,0:T(8,128)(2,1)}) %all-gather.13.cloned.1.call-update) | async-done | bytes 2097168 | tf_op jit(solution)/shard_map/all_gather | solution.py:37
  186.5 0.0 copy-start.4
  186.5 2.4 fusion.7
  188.8 0.0 copy-done.4
  188.8 0.4 convolution_bitcast_fusion
  189.2 0.0 copy-start.5
  189.3 0.4 convolution_bitcast_fusion.1
  189.7 0.4 convolution_bitcast_fusion.2
  190.1 0.2 copy-done.5
  190.3 0.0 copy-start.8
  190.3 0.0 copy-start.9
  190.3 0.0 copy-start.10
  190.3 2.7 fusion.18
  193.0 0.0 reduce-scatter.2.cloned.1.call-update
  193.0 22.0 %psum.7 = s32[]{:T(128)} all-reduce(s32[]{:T(128)} %get-tuple-element.13), channel_id=1, replica_groups=mesh['dp'=64,'tensor'=8] {'dp'}, use_global_device_ids=true, to_apply=%region_1.0 | all-reduce | flops 1 | bytes 8 | tf_op jit(solution)/shard_map/psum | solution.py:41
  216.4 798.4 %reduce-scatter.2.cloned.1.call-done = f32[3,16,128]{2,1,0:T(8,128)} async-done(((f32[3,16,8192]{2,1,0:T(8,128)}), f32[3,16,128]{2,1,0:T(8,128)}) %reduce-scatter.2.cloned.1.call-update) | async-done | bytes 24592 | tf_op jit(solution)/shard_map/reduce_scatter | solution.py:42
  1014.8 0.0 copy-done.8
  1014.8 0.0 copy-done.9
  1014.8 0.0 copy-done.10
  1014.8 1.4 multiply_subtract_fusion
Async XLA Ops:
  7.2 48.8 %copy-start = (bf16[8192,16]{0,1:T(8,128)(2,1)S(1)}, bf16[8192,16]{0,1:T(8,128)(2,1)}, u32[]{:S(2)}) copy-start(bf16[8192,16]{0,1:T(8,128)(2,1)} %param.13) | copy-start | bytes 786436
  7.2 5.3 copy-start.11
  7.2 48.8 %all-gather.11.cloned.1.call-start = ((), (), s32[]{:S(2)}) async-start(), calls=%async_computation.3 | async-start | bytes 2359296 | tf_op jit(solution)/shard_map/all_gather | solution.py:36
  9.1 49.2 %copy-start.6 = (bf16[8192,16]{0,1:T(8,128)(2,1)S(1)}, bf16[8192,16]{0,1:T(8,128)(2,1)}, u32[]{:S(2)}) copy-start(bf16[8192,16]{0,1:T(8,128)(2,1)} %param.12) | copy-start | bytes 786436
  9.2 90.3 %all-gather.9.cloned.1.call-start = ((), (), s32[]{:S(2)}) async-start(), calls=%async_computation.2 | async-start | bytes 2359296 | tf_op jit(solution)/shard_map/all_gather | solution.py:37
  11.2 131.9 %all-gather.15.cloned.1.call-start = ((), (), s32[]{:S(2)}) async-start(), calls=%async_computation.5 | async-start | bytes 2359296 | tf_op jit(solution)/shard_map/all_gather | solution.py:36
  11.9 174.6 %all-gather.13.cloned.1.call-start = ((), (), s32[]{:S(2)}) async-start(), calls=%async_computation.4 | async-start | bytes 2359296 | tf_op jit(solution)/shard_map/all_gather | solution.py:37
  12.5 1002.3 %reduce-scatter.2.cloned.1.call-start = ((), (), s32[]{:S(2)}) async-start(), calls=%async_computation.1 | async-start | bytes 1597440 | tf_op jit(solution)/shard_map/reduce_scatter | solution.py:42
  56.0 2.4 copy-start.1
  58.4 43.3 %copy-start.7 = (bf16[16,8192]{1,0:T(8,128)(2,1)S(1)}, bf16[16,8192]{1,0:T(8,128)(2,1)}, u32[]{:S(2)}) copy-start(bf16[16,8192]{1,0:T(8,128)(2,1)} %param.14) | copy-start | bytes 786436
  99.5 2.2 copy-start.3
  143.1 2.4 copy-start.2
  186.5 2.4 copy-start.4
  189.2 1.1 copy-start.5
  190.3 824.5 %copy-start.8 = (f32[3,16,128]{2,1,0:T(8,128)S(1)}, f32[3,16,128]{2,1,0:T(8,128)}, u32[]{:S(2)}) copy-start(f32[3,16,128]{2,1,0:T(8,128)} %param.17) | copy-start | bytes 73732
  190.3 824.5 %copy-start.9 = (f32[3,16,128]{2,1,0:T(8,128)S(1)}, f32[3,16,128]{2,1,0:T(8,128)}, u32[]{:S(2)}) copy-start(f32[3,16,128]{2,1,0:T(8,128)} %param.19) | copy-start | bytes 73732
  190.3 824.5 %copy-start.10 = (f32[3,16,128]{2,1,0:T(8,128)S(1)}, f32[3,16,128]{2,1,0:T(8,128)}, u32[]{:S(2)}) copy-start(f32[3,16,128]{2,1,0:T(8,128)} %param.18) | copy-start | bytes 73732
Sparse Core Ops, SparseCore 0:
  10.1 45.8 all-gather.10
  58.0 41.3 all-gather.8
  101.6 41.4 all-gather.14
  145.0 41.3 all-gather.12
  193.1 821.6 reduce-scatter.1
where the time goes:
time: 1030 us; the launch traced here: 1020 us
  waiting for transfers between devices  961 us (93%)
  blocking collectives  22 us (2%)
  between operations  15.2 us (1%)
  matrix products  15 us (1%)
    reduce_scatter x1, waiting for transfers between devices, per_device(): summed = lax.psum_scatter(total, 'dp', scatter_dimension=2, tiled=True)  798 us
    all_gather x2, waiting for transfers between devices, per_device(): lax.all_gather(acts[index], 'tensor', axis=0, tiled=True)  81.3 us
    all_gather x2, waiting for transfers between devices, per_device(): lax.all_gather(grad_out[index], 'tensor', axis=0, tiled=True)  79.8 us
    psum x1, blocking collectives, per_device(): count = lax.psum(local_count, 'dp').astype(jnp.float32)  22 us
  transfers between devices with their start and end apart: 5, of which 5 were waited for; matrix products, arithmetic and copies ran while one was open for 1% of the time, Pallas kernels for 0%

commit v1 on v0

v1 whole, which is shorter than its diff:
```python
import jax
import jax.numpy as jnp
from jax import lax
from jax.experimental import pallas as pl
from jax.experimental.pallas import tpu as pltpu
from jax.sharding import PartitionSpec as P

X, YH, YL, Z = 4, 2, 4, 8
Y = YH * YL
C = 2
MB, RT = 2, 16
TOK = MB * RT
SLOTS = X * C
LANES = 128
CC = Z * LANES
HID = 128
MESH = pl.DeviceIdType.MESH
NT = (((1,), (1,)), ((), ()))


def dev(y, z, x, c):
    return (lax.div(y, YL) * Z + z) * X + x, lax.rem(y, YL) * C + c


def kernel(
    acts_hbm, dy_hbm, wg_hbm, wu_hbm, wd_hbm, ovf, out,
    acts_v, dy_v, w_v, sx, bx, sw, wb, pt, rx, ab, sz, rz, sy, ry, s2y, r2y, s2z, r2z,
    ld, xs, xr, ws, wr, ps, pr, as_, ar, zs, zr, ys, yr, y2s, y2r, z2s, z2r,
):
    dp, t = lax.axis_index("dp"), lax.axis_index("tensor")
    x = lax.rem(dp, X)
    z = lax.rem(lax.div(dp, X), Z)
    yh = lax.div(dp, X * Z)
    yl = lax.div(t, C)
    c = lax.rem(t, C)
    y = yh * YL + yl
    me = x * C + c
    sib = 1 - c

    loads = [
        pltpu.make_async_copy(src, dst, ld.at[i])
        for i, (src, dst) in enumerate(
            [(acts_hbm, acts_v), (dy_hbm, dy_v), (wg_hbm, w_v.at[0]), (wu_hbm, w_v.at[1]), (wd_hbm, w_v.at[2])]
        )
    ]
    for load in loads:
        load.start()

    barrier = pltpu.get_barrier_semaphore()
    friends = []
    for dx in range(X):
        for dc in range(C):
            if dx or dc:
                friends.append(dev(y, z, lax.rem(x + dx, X), lax.rem(c + dc, C)))
    for step in range(1, Y):
        for dc in range(C):
            friends.append(dev(lax.rem(y + step, Y), z, x, lax.rem(c + dc, C)))
    for step in range(1, Z):
        friends.append(dev(y, lax.rem(z + step, Z), x, c))
    for friend in friends:
        pl.semaphore_signal(barrier, inc=1, device_id=friend, device_id_type=MESH)
    for load in loads:
        load.wait()
    pl.semaphore_wait(barrier, len(friends))

    sends = []

    def send(src, dst, send_sem, recv_sem, where):
        copy = pltpu.make_async_remote_copy(
            src_ref=src, dst_ref=dst, send_sem=send_sem, recv_sem=recv_sem, device_id=where, device_id_type=MESH
        )
        copy.start()
        return copy

    def arrived(dst, sem):
        pltpu.make_async_copy(dst, dst, sem).wait()

    def gather_columns(store, xp, cp):
        for k in range(Z):
            at = pl.ds(pl.multiple_of(((cp * Z + k) * X + xp) * LANES, LANES), LANES)
            store(0, k, acts_v[:, :, at])
            store(1, k, dy_v[:, :, at])

    for dx in [2, 1, 3, 0] if X == 4 else list(range(1, X)) + [0]:
        for dc in range(C):
            if dx == 0 and dc == 0:
                continue
            xp, cp = lax.rem(x + dx, X), lax.rem(c + dc, C)
            n = dx * C + dc

            def store(a, k, value, n=n):
                sx[n, a, :, :, k * LANES : (k + 1) * LANES] = value

            gather_columns(store, xp, cp)
            sends.append(send(sx.at[n], bx.at[:, me], xs.at[n], xr.at[n], dev(y, z, xp, cp)))

    for cp in range(C):
        for k in range(Z):
            at = pl.ds(pl.multiple_of(((cp * Z + k) * X + x) * LANES, LANES), LANES)
            sw[cp, :, :, k * LANES : (k + 1) * LANES] = w_v[:, :, at]
    rows = pl.ds(pl.multiple_of(t * RT, RT), RT)
    half = CC // 2
    hops = [
        (1, slice(0, CC)),
        (Y - 1, slice(0, CC)),
        (2, slice(0, half)),
        (Y - 2, slice(half, CC)),
    ]
    for i, (hop, cols) in enumerate(hops):
        for cp in range(C):
            sends.append(
                send(
                    sw.at[cp, :, :, cols],
                    wb.at[:, rows, cols],
                    ws.at[i * C + cp],
                    wr.at[i * C + c],
                    dev(lax.rem(y + hop, Y), z, x, cp),
                )
            )
    n = len(hops) * C
    sends.append(send(sw.at[sib], wb.at[:, rows, :], ws.at[n], wr.at[n], dev(y, z, x, sib)))
    wb[:, rows, :] = sw[c]

    def store(a, k, value):
        bx[a, me, :, :, k * LANES : (k + 1) * LANES] = value

    gather_columns(store, x, c)

    for i, (hop, cols) in enumerate(hops):
        for cp in range(C):
            arrived(wb.at[:, rows, cols], wr.at[i * C + cp])
    arrived(wb.at[:, rows, :], wr.at[n])

    lost = (ovf[0, 0] + ovf[0, 1]).astype(jnp.float32)
    for dx in [0, 1, 3, 2] if X == 4 else range(X):
        for dc in range(C):
            if dx or dc:
                arrived(bx.at[:, me], xr.at[dx * C + dc])
        g = lax.rem(x - dx + X, X)
        a = bx[0, pl.ds(g * C, C)].reshape(C * TOK, CC)
        d = bx[1, pl.ds(g * C, C)].reshape(C * TOK, CC)
        gate_up = lax.dot_general(a, wb[0:2].reshape(2 * HID, CC), NT, preferred_element_type=jnp.float32)
        dh = lax.dot_general(d, wb[2], NT, preferred_element_type=jnp.float32)
        for cc in range(C):
            part = slice(cc * TOK, (cc + 1) * TOK)
            pt[g * C + cc, 0:TOK] = gate_up[part, :HID]
            pt[g * C + cc, TOK : 2 * TOK] = gate_up[part, HID:]
            pt[g * C + cc, 2 * TOK : 3 * TOK] = dh[part]
            pt[g * C + cc, 3 * TOK :] = jnp.full((8, LANES), lost, jnp.float32)
        for dc in range(C):
            if dx or dc:
                cp = lax.rem(c + dc, C)
                n = dx * C + dc
                sends.append(send(pt.at[g * C + cp], rx.at[me], ps.at[n], pr.at[n], dev(y, z, g, cp)))
    rx[me] = pt[me]
    for n in range(1, SLOTS):
        arrived(rx.at[me], pr.at[n])
    total = rx[0]
    for n in range(1, SLOTS):
        total = total + rx[n]
    gate, up, dh = total[0:TOK], total[TOK : 2 * TOK], total[2 * TOK : 3 * TOK]
    count = total[3 * TOK :]
    sig = 1.0 / (1.0 + jnp.exp(-gate))
    silu = gate * sig
    first = lax.broadcasted_iota(jnp.int32, (TOK, HID), 0) < RT
    keep_rows = jnp.where(first, 1 - ovf[0, 0], 1 - ovf[0, 1]) > 0
    zero = jnp.zeros((TOK, HID), jnp.float32)
    ab[me, 0] = jnp.where(keep_rows, dh * up * sig * (1.0 + gate * (1.0 - sig)), zero).astype(jnp.bfloat16)
    ab[me, 1] = jnp.where(keep_rows, dh * silu, zero).astype(jnp.bfloat16)
    ab[me, 2] = jnp.where(keep_rows, silu * up, zero).astype(jnp.bfloat16)
    for dx in range(X):
        for dc in range(C):
            if dx or dc:
                n = dx * C + dc
                where = dev(y, z, lax.rem(x + dx, X), lax.rem(c + dc, C))
                sends.append(send(ab.at[me], ab.at[me], as_.at[n], ar.at[n], where))
    for n in range(1, SLOTS):
        arrived(ab.at[me], ar.at[n])

    lhs = [jnp.transpose(ab[:, k].reshape(SLOTS * TOK, HID)) for k in range(3)]
    lhs_gu = jnp.concatenate(lhs[:2], axis=0)
    wide = 2 * LANES
    for zt in range(Z // 2):
        cols = slice(zt * wide, (zt + 1) * wide)
        acts_cols = bx[0, :, :, :, cols].reshape(SLOTS * TOK, wide)
        dy_cols = bx[1, :, :, :, cols].reshape(SLOTS * TOK, wide)
        gu = jnp.dot(lhs_gu, acts_cols, preferred_element_type=jnp.float32)
        dn = jnp.dot(lhs[2], dy_cols, preferred_element_type=jnp.float32)
        for k, block in enumerate([gu[:HID], gu[HID:], dn]):
            pair = [block[:, :LANES], block[:, LANES:]]
            for b in range(2):
                low = [pair[b][i * RT : i * RT + 8] for i in range(YL * C)]
                sz[zt * 2 + b, k * 64 : (k + 1) * 64] = jnp.concatenate(low, axis=0).astype(jnp.bfloat16)
            for i in range(YL * C):
                high = [p[i * RT + 8 : (i + 1) * RT] for p in pair]
                at = k * 8 * Z + zt * 16
                sy[i, at : at + 16] = jnp.concatenate(high, axis=0).astype(jnp.bfloat16)
    for k in range(Z):
        sz[k, 192:208] = jnp.concatenate([count, count], axis=0).astype(jnp.bfloat16)

    same = c == yh

    def to_y(buf, slots, send_sems, recv_sems):
        for rel in range(1, YL * C):
            i = lax.rem(t + rel, YL * C)
            where = dev(c * YL + lax.div(i, C), z, x, lax.rem(i, C))
            sends.append(send(buf.at[i], slots.at[y], send_sems.at[rel], recv_sems.at[y], where))

        @pl.when(same)
        def _():
            slots[y] = buf[t]

        @pl.when(jnp.logical_not(same))
        def _():
            send(buf.at[t], slots.at[y], send_sems.at[0], recv_sems.at[y], dev(c * YL + yl, z, x, c))

    def from_y(buf, slots, send_sems, recv_sems):
        for rel in range(1, Y):
            arrived(slots.at[y], recv_sems.at[lax.rem(y + rel, Y)])

        @pl.when(jnp.logical_not(same))
        def _():
            arrived(slots.at[y], recv_sems.at[y])
            pltpu.make_async_copy(buf.at[t], buf.at[t], send_sems.at[0]).wait()

    def to_z(buf, slots, send_sems, recv_sems):
        for rel in range(1, Z):
            zp = lax.rem(z + rel, Z)
            sends.append(send(buf.at[zp], slots.at[z], send_sems.at[rel], recv_sems.at[rel], dev(y, zp, x, c)))
        slots[z] = buf[z]

    def from_z(slots, recv_sems):
        for rel in range(1, Z):
            arrived(slots.at[z], recv_sems.at[rel])

    def added(slots, length):
        value = slots[0].astype(jnp.float32)
        for n in range(1, length):
            value = value + slots[n].astype(jnp.float32)
        return value

    to_y(sy, ry, ys, yr)
    to_z(sz, rz, zs, zr)
    from_y(sy, ry, ys, yr)
    high = added(ry, Y)
    for k in range(Z):
        for m in range(3):
            at = m * 8 * Z + k * 8
            s2z[k, m * 8 : (m + 1) * 8] = high[at : at + 8]
    to_z(s2z, r2z, z2s, z2r)
    from_z(rz, zr)
    low = added(rz, Z)
    for i in range(YL * C):
        for m in range(3):
            s2y[i, m * 8 : (m + 1) * 8] = low[m * 64 + i * 8 : m * 64 + (i + 1) * 8]
        s2y[i, 24:32] = low[192:200]
    to_y(s2y, r2y, y2s, y2r)
    from_z(r2z, z2r)
    high = added(r2z, Z)
    from_y(s2y, r2y, y2s, y2r)
    low = added(r2y, Y)
    for m in range(3):
        out[m * 16 : m * 16 + 8] = low[m * 8 : (m + 1) * 8]
        out[m * 16 + 8 : (m + 1) * 16] = high[m * 8 : (m + 1) * 8]
    out[48:56] = low[24:32]

    for copy in sends:
        copy.wait_send()


def reduced_grads(acts, grad_out, w_gate, w_up, w_down, overflow):
    d = acts.shape[2]
    bf16, f32 = jnp.bfloat16, jnp.float32
    hbm = pl.BlockSpec(memory_space=pl.ANY)
    dma = pltpu.SemaphoreType.DMA
    return pl.pallas_call(
        kernel,
        out_shape=jax.ShapeDtypeStruct((56, LANES), f32),
        in_specs=[hbm] * 5 + [pl.BlockSpec(memory_space=pltpu.SMEM)],
        out_specs=pl.BlockSpec(memory_space=pltpu.VMEM),
        scratch_shapes=[
            pltpu.VMEM((MB, RT, d), bf16),
            pltpu.VMEM((MB, RT, d), bf16),
            pltpu.VMEM((3, RT, d), bf16),
            pltpu.VMEM((SLOTS, 2, MB, RT, CC), bf16),
            pltpu.VMEM((2, SLOTS, MB, RT, CC), bf16),
            pltpu.VMEM((C, 3, RT, CC), bf16),
            pltpu.VMEM((3, HID, CC), bf16),
            pltpu.VMEM((SLOTS, 3 * TOK + 8, LANES), f32),
            pltpu.VMEM((SLOTS, 3 * TOK + 8, LANES), f32),
            pltpu.VMEM((SLOTS, 3, TOK, HID), bf16),
            pltpu.VMEM((Z, 208, LANES), bf16),
            pltpu.VMEM((Z, 208, LANES), bf16),
            pltpu.VMEM((YL * C, 24 * Z, LANES), bf16),
            pltpu.VMEM((Y, 24 * Z, LANES), bf16),
            pltpu.VMEM((YL * C, 32, LANES), f32),
            pltpu.VMEM((Y, 32, LANES), f32),
            pltpu.VMEM((Z, 24, LANES), f32),
            pltpu.VMEM((Z, 24, LANES), f32),
            dma((5,)),
            dma((SLOTS,)), dma((SLOTS,)),
            dma((9,)), dma((9,)),
            dma((SLOTS,)), dma((SLOTS,)),
            dma((SLOTS,)), dma((SLOTS,)),
            dma((Z,)), dma((Z,)),
            dma((Y,)), dma((Y,)),
            dma((Y,)), dma((Y,)),
            dma((Z,)), dma((Z,)),
        ],
        compiler_params=pltpu.CompilerParams(
            collective_id=0, has_side_effects=True, vmem_limit_bytes=40 * 1024 * 1024
        ),
        name="window_grads",
    )(acts, grad_out, w_gate.T, w_up.T, w_down, overflow)


def per_device(acts, grad_out, w_gate, w_up, w_down, overflow, step, master, moment1, moment2):
    n_dp = lax.axis_size("dp")
    micro = acts.shape[0]
    reduced = reduced_grads(acts, grad_out, w_gate, w_up, w_down, overflow)
    grad = reduced[:48].reshape(master.shape) / jnp.float32(micro * n_dp)
    count = reduced[48, 0] * jnp.float32(1.0 / (C * YL))
    keep = 1.0 - count / jnp.float32(micro * n_dp)
    new_moment1 = 0.9 * moment1 + 0.1 * grad
    new_moment2 = 0.95 * moment2 + 0.05 * grad * grad
    steps_f = step[0].astype(jnp.float32)
    corr1 = 1.0 - jnp.power(jnp.float32(0.9), steps_f)
    corr2 = 1.0 - jnp.power(jnp.float32(0.95), steps_f)
    direction = new_moment1 / corr1 / (jnp.sqrt(new_moment2 / corr2) + 1e-08)
    new_master = master - 0.01 * keep * (direction + 0.1 * master)
    return (new_master, new_moment1, new_moment2)


def solution(mesh):
    in_specs = (
        P(None, ("dp", "tensor"), None),
        P(None, ("dp", "tensor"), None),
        P(None, "tensor"),
        P(None, "tensor"),
        P("tensor", None),
        P("dp", None),
        P(),
        P(None, "tensor", "dp"),
        P(None, "tensor", "dp"),
        P(None, "tensor", "dp"),
    )
    out_specs = (P(None, "tensor", "dp"), P(None, "tensor", "dp"), P(None, "tensor", "dp"))
    return jax.shard_map(
        per_device, mesh=mesh, in_specs=in_specs, out_specs=out_specs, check_vma=False
    )
```

time: 1030 us -> 70.1 us (0.07)
  waiting for transfers between devices: 961 us -> 0 us
  Pallas kernels: 0 us -> 60.1 us
  blocking collectives: 22 us -> 0 us
  matrix products: 15 us -> 0 us
  between operations: 15.2 us -> 2.07 us
    reduce_scatter x1 -> x0, waiting for transfers between devices: 798 us -> none  [per_device(): summed = lax.psum_scatter(total, 'dp', scatter_dimension=2, tiled=True)]
    all_gather x4 -> x0, waiting for transfers between devices: 161 us -> none  [the longest x2 81.3 us: per_device(): lax.all_gather(acts[index], 'tensor', axis=0, tiled=True)]
    pallas_call x0 -> x1, Pallas kernels: none -> 60.1 us  [reduced_grads(): pl.pallas_call(kernel, out_shape=jax.ShapeDtypeStruct((56, LANES), f32),...]
    psum x1 -> x0, blocking collectives: 22 us -> none  [per_device(): count = lax.psum(local_count, 'dp').astype(jnp.float32)]
    dot_general x12 -> x0, matrix products: 15 us -> none  [the longest x6 4.97 us: contract_rows(): lax.dot_general(left, right, (((0,), (0,)), ((), ())), preferred_element_...]
  transfers between devices with their start and end apart: 5 -> 0, of which waited for: 5 -> 0; matrix products, arithmetic and copies ran while one was open for 1% -> 0% of each run, Pallas kernels for 0% -> 0%
where the time goes in v1:
time: 70.1 us; the launch traced here: 69.7 us
  Pallas kernels  60.1 us (86%)
  local copies, waits for them, and re-layouts  6.83 us (10%)
  between operations  2.07 us (3%)
    pallas_call x1, Pallas kernels, reduced_grads(): pl.pallas_call(kernel, out_shape=jax.ShapeDtypeStruct((56, LANES), f32),...  60.1 us
    unnamed x18, local copies, waits for them, and re-layouts  6.31 us

profile of v1, /device:TPU:1, one launch (start us, length us, event | category | flops | bytes accessed | tf_op | source)
XLA Modules:
  0.0 69.7 jit_solution(18226973067251975538)
XLA Ops:
  1.4 0.0 copy-start.5
  1.4 0.6 copy-done.5
  2.0 0.0 copy-start
  2.0 1.0 %copy-done = bf16[2,16,8192]{2,1,0:T(8,128)(2,1)S(1)} copy-done((bf16[2,16,8192]{2,1,0:T(8,128)(2,1)S(1)}, bf16[2,16,8192]{2,1,0:T(8,128)(2,1)}, u32[]{:S(2)}) %copy-start) | copy-done | bytes 524312
  3.1 0.0 copy-start.1
  3.1 1.0 %copy-done.1 = bf16[2,16,8192]{2,1,0:T(8,128)(2,1)S(1)} copy-done((bf16[2,16,8192]{2,1,0:T(8,128)(2,1)S(1)}, bf16[2,16,8192]{2,1,0:T(8,128)(2,1)}, u32[]{:S(2)}) %copy-start.1) | copy-done | bytes 524312
  4.1 0.0 copy-start.2
  4.1 0.9 %copy-done.2 = bf16[8192,16]{0,1:T(8,128)(2,1)S(1)} copy-done((bf16[8192,16]{0,1:T(8,128)(2,1)S(1)}, bf16[8192,16]{0,1:T(8,128)(2,1)}, u32[]{:S(2)}) %copy-start.2) | copy-done | bytes 262168
  5.1 0.0 copy-start.3
  5.1 0.9 %copy-done.3 = bf16[8192,16]{0,1:T(8,128)(2,1)S(1)} copy-done((bf16[8192,16]{0,1:T(8,128)(2,1)S(1)}, bf16[8192,16]{0,1:T(8,128)(2,1)}, u32[]{:S(2)}) %copy-start.3) | copy-done | bytes 262168
  6.0 0.0 copy-start.4
  6.0 0.9 %copy-done.4 = bf16[16,8192]{1,0:T(8,128)(2,1)S(1)} copy-done((bf16[16,8192]{1,0:T(8,128)(2,1)S(1)}, bf16[16,8192]{1,0:T(8,128)(2,1)}, u32[]{:S(2)}) %copy-start.4) | copy-done | bytes 262168
  7.0 60.1 %window_grads.1 = f32[56,128]{1,0:T(8,128)S(1)} custom-call(bf16[2,16,8192]{2,1,0:T(8,128)(2,1)S(1)} %copy-done, bf16[2,16,8192]{2,1,0:T(8,128)(2,1)S(1)} %copy-done.1, bf16[16,8192]{1,0:T(8,128)(2,1)S(1)} %bitcast.7, bf16[16,8192]{1,0:T(8,128)(2,1)S(1)} %bitcast.8, bf16[16,8192]{1,0:T(8,128)(2,1)S(1)} %copy-done.4, s32[1,2]{1,0:T(1,128)S(1)} %copy-done.5), custom_call_target="tpu_custom_call" | custom-call | tf_op jit(solution)/shard_map/window_grads/pallas_call | solution.py:276
  67.1 0.5 slice.6
  68.3 0.0 copy-start.6
  68.3 0.0 copy-start.7
  68.3 0.0 copy-start.8
  68.3 0.7 copy-done.6
  69.0 0.0 copy-done.7
  69.0 0.0 copy-done.8
  69.0 0.6 multiply_subtract_fusion
  (1 shorter events, 0.0 us)
Async XLA Ops:
  1.4 0.7 copy-start.5
  2.0 1.0 %copy-start = (bf16[2,16,8192]{2,1,0:T(8,128)(2,1)S(1)}, bf16[2,16,8192]{2,1,0:T(8,128)(2,1)}, u32[]{:S(2)}) copy-start(bf16[2,16,8192]{2,1,0:T(8,128)(2,1)} %acts_hbm.1) | copy-start | bytes 1572868
  3.1 1.0 %copy-start.1 = (bf16[2,16,8192]{2,1,0:T(8,128)(2,1)S(1)}, bf16[2,16,8192]{2,1,0:T(8,128)(2,1)}, u32[]{:S(2)}) copy-start(bf16[2,16,8192]{2,1,0:T(8,128)(2,1)} %dy_hbm.1) | copy-start | bytes 1572868
  4.1 0.9 %copy-start.2 = (bf16[8192,16]{0,1:T(8,128)(2,1)S(1)}, bf16[8192,16]{0,1:T(8,128)(2,1)}, u32[]{:S(2)}) copy-start(bf16[8192,16]{0,1:T(8,128)(2,1)} %param.12) | copy-start | bytes 786436
  5.1 0.9 %copy-start.3 = (bf16[8192,16]{0,1:T(8,128)(2,1)S(1)}, bf16[8192,16]{0,1:T(8,128)(2,1)}, u32[]{:S(2)}) copy-start(bf16[8192,16]{0,1:T(8,128)(2,1)} %param.13) | copy-start | bytes 786436
  6.0 0.9 %copy-start.4 = (bf16[16,8192]{1,0:T(8,128)(2,1)S(1)}, bf16[16,8192]{1,0:T(8,128)(2,1)}, u32[]{:S(2)}) copy-start(bf16[16,8192]{1,0:T(8,128)(2,1)} %wd_hbm.1) | copy-start | bytes 786436
  68.3 0.7 %copy-start.6 = (f32[3,16,128]{2,1,0:T(8,128)S(1)}, f32[3,16,128]{2,1,0:T(8,128)}, u32[]{:S(2)}) copy-start(f32[3,16,128]{2,1,0:T(8,128)} %param.17) | copy-start | bytes 73732
  68.3 0.7 %copy-start.7 = (f32[3,16,128]{2,1,0:T(8,128)S(1)}, f32[3,16,128]{2,1,0:T(8,128)}, u32[]{:S(2)}) copy-start(f32[3,16,128]{2,1,0:T(8,128)} %param.19) | copy-start | bytes 73732
  68.3 0.8 %copy-start.8 = (f32[3,16,128]{2,1,0:T(8,128)S(1)}, f32[3,16,128]{2,1,0:T(8,128)}, u32[]{:S(2)}) copy-start(f32[3,16,128]{2,1,0:T(8,128)} %param.18) | copy-start | bytes 73732

commit v2 on v0

v2 whole, which is shorter than its diff:
```python
import jax
import jax.numpy as jnp
from jax import lax
from jax.experimental import pallas as pl
from jax.experimental.pallas import tpu as pltpu
from jax.sharding import PartitionSpec as P

X, YH, YL, Z = 4, 2, 4, 8
Y = YH * YL
C = 2
MB, RT = 2, 16
TOK = MB * RT
SLOTS = 4 * C
LANES = 128
BLOCKS = (X // 2) * (Z // 2)
CC = BLOCKS * LANES
HID = 128
MESH = pl.DeviceIdType.MESH
NT = (((1,), (1,)), ((), ()))


def dev(y, z, x, c):
    return (lax.div(y, YL) * Z + z) * X + x, lax.rem(y, YL) * C + c


def kernel(
    acts_hbm, dy_hbm, wg_hbm, wu_hbm, wd_hbm, ovf_hbm, out, rate_out,
    ovf, acts_v, dy_v, w_v, sx, sd, bx, bd, sw, wb, pt, pd, rx, rd, ab, hb, sz, rz, sy, ry, s2y, r2y, s2z, r2z,
    n1, m2, m3, ld, xs, xr, ds, dr, ws, wr, ps, pr, qs, qr, as_, ar, hs, hr, zs, zr, ys, yr, y2s, y2r, z2s, z2r,
    n1s, n1r, n2s, n2r, n3s, n3r,
):
    dp, t = lax.axis_index("dp"), lax.axis_index("tensor")
    x = lax.rem(dp, X)
    z = lax.rem(lax.div(dp, X), Z)
    yh = lax.div(dp, X * Z)
    yl = lax.div(t, C)
    c = lax.rem(t, C)
    y = yh * YL + yl
    sib = 1 - c
    px, pz = lax.rem(x, 2), lax.rem(z, 2)
    me = (px * 2 + pz) * C + c
    kme = lax.div(z, 2) * (X // 2) + lax.div(x, 2)

    even_x, even_z = x + 1 - 2 * px, z + 1 - 2 * pz
    odd_x, odd_z = lax.rem(x + X - 1 + 2 * px, X), lax.rem(z + Z - 1 + 2 * pz, Z)

    def even(ex, ez, core):
        return dev(y, even_z if ez else z, even_x if ex else x, core)

    def odd(ex, ez, core):
        return dev(y, odd_z if ez else z, odd_x if ex else x, core)

    def across(bit, flip):
        return 1 - bit if flip else bit

    def slot(ex, ez, ec):
        return (across(px, ex) * 2 + across(pz, ez)) * C + across(c, ec)

    def number(ex, ez, ec):
        return (ex * 2 + ez) * C + ec

    others = [(1, 1, 0), (1, 1, 1), (1, 0, 0), (0, 1, 0), (1, 0, 1), (0, 1, 1), (0, 0, 1)]

    loads = [
        pltpu.make_async_copy(src, dst, ld.at[i])
        for i, (src, dst) in enumerate(
            [
                (wg_hbm, w_v.at[0]),
                (wu_hbm, w_v.at[1]),
                (wd_hbm, w_v.at[2]),
                (acts_hbm, acts_v),
                (dy_hbm, dy_v),
                (ovf_hbm, ovf),
            ]
        )
    ]
    for load in loads:
        load.start()

    barrier = pltpu.get_barrier_semaphore()
    friends = [even(ex, ez, across(c, ec)) for ex, ez, ec in others]
    friends += [odd(ex, ez, across(c, ec)) for ex, ez, ec in others if ex or ez]
    for step in range(1, Y):
        for dc in range(C):
            friends.append(dev(lax.rem(y + step, Y), z, x, across(c, dc)))

    def class_dev(k):
        return dev(y, lax.div(k, X // 2) * 2 + pz, lax.rem(k, X // 2) * 2 + px, c)

    for step in range(1, BLOCKS):
        friends.append(class_dev(lax.rem(kme + step, BLOCKS)))
    for friend in friends:
        pl.semaphore_signal(barrier, inc=1, device_id=friend, device_id_type=MESH)

    def columns(k, qx, qz, core):
        kz, kx = k // (X // 2), k % (X // 2)
        block = (core * Z + 2 * kz + qz) * X + 2 * kx + qx
        return pl.ds(pl.multiple_of(block * LANES, LANES), LANES)

    for load in loads[:3]:
        load.wait()
    for cp in range(C):
        for k in range(BLOCKS):
            sw[cp, :, :, k * LANES : (k + 1) * LANES] = w_v[:, :, columns(k, px, pz, cp)]
    pl.semaphore_wait(barrier, len(friends))

    sends = []

    def send(src, dst, send_sem, recv_sem, where):
        copy = pltpu.make_async_remote_copy(
            src_ref=src, dst_ref=dst, send_sem=send_sem, recv_sem=recv_sem, device_id=where, device_id_type=MESH
        )
        copy.start()
        return copy

    def arrived(dst, sem):
        pltpu.make_async_copy(dst, dst, sem).wait()

    same = c == yh

    def to_y(buf, slots, send_sems, recv_sems):
        for rel in range(1, YL * C):
            i = lax.rem(t + rel, YL * C)
            where = dev(c * YL + lax.div(i, C), z, x, lax.rem(i, C))
            sends.append(send(buf.at[i], slots.at[y], send_sems.at[rel], recv_sems.at[y], where))

        @pl.when(same)
        def _():
            slots[y] = buf[t]

        @pl.when(jnp.logical_not(same))
        def _():
            send(buf.at[t], slots.at[y], send_sems.at[0], recv_sems.at[y], dev(c * YL + yl, z, x, c))

    def from_y(buf, slots, send_sems, recv_sems):
        for rel in range(1, Y):
            arrived(slots.at[y], recv_sems.at[lax.rem(y + rel, Y)])

        @pl.when(jnp.logical_not(same))
        def _():
            arrived(slots.at[y], recv_sems.at[y])
            pltpu.make_async_copy(buf.at[t], buf.at[t], send_sems.at[0]).wait()

    def to_z(buf, slots, send_sems, recv_sems):
        for rel in range(1, BLOCKS):
            k = lax.rem(kme + rel, BLOCKS)
            sends.append(send(buf.at[k], slots.at[kme], send_sems.at[rel], recv_sems.at[kme], class_dev(k)))
        slots[kme] = buf[kme]

    def from_z(slots, recv_sems):
        for rel in range(1, BLOCKS):
            arrived(slots.at[kme], recv_sems.at[lax.rem(kme + rel, BLOCKS)])

    def added(slots, length):
        value = slots[0].astype(jnp.float32)
        for n in range(1, length):
            value = value + slots[n].astype(jnp.float32)
        return value

    rows = pl.ds(pl.multiple_of(t * RT, RT), RT)
    half = CC // 2
    one, two = slice(0, half), slice(half, CC)
    routes = [(Y - 1, one), (1, two), (Y - 1, two), (1, one)]
    for i, (hop, cols) in enumerate(routes):
        for cp in range(C):
            where = dev(lax.rem(y + hop, Y), z, x, cp)
            sends.append(send(sw.at[cp, :, :, cols], wb.at[:, rows, cols], ws.at[i * C + cp], wr.at[i * C + c], where))
    sends.append(send(sw.at[sib], wb.at[:, rows, :], ws.at[8], wr.at[8], dev(y, z, x, sib)))
    for load in loads[3:]:
        load.wait()
    for ex, ez, ec in others:
        n = number(ex, ez, ec)
        for k in range(BLOCKS):
            at = columns(k, across(px, ex), across(pz, ez), across(c, ec))
            sx[n, :, :, k * LANES : (k + 1) * LANES] = acts_v[:, :, at]
            sd[n, :, :, k * LANES : (k + 1) * LANES] = dy_v[:, :, at]
        sends.append(send(sx.at[n], bx.at[me], xs.at[n], xr.at[n], even(ex, ez, across(c, ec))))
        sends.append(send(sd.at[n], bd.at[me], ds.at[n], dr.at[n], odd(ex, ez, across(c, ec))))
    lost = (ovf[0, 0] + ovf[0, 1]).astype(jnp.float32)
    square = px * 2 + pz
    n1[square] = jnp.full((8, LANES), lost, jnp.float32)
    for n, (ex, ez) in enumerate([(1, 1), (1, 0), (0, 1)]):
        sends.append(send(n1.at[square], n1.at[square], n1s.at[n], n1r.at[n], even(ex, ez, c)))
    wb[:, rows, :] = sw[c]
    for k in range(BLOCKS):
        at = columns(k, px, pz, c)
        bx[me, :, :, k * LANES : (k + 1) * LANES] = acts_v[:, :, at]
        bd[me, :, :, k * LANES : (k + 1) * LANES] = dy_v[:, :, at]

    for i, (hop, cols) in enumerate(routes[:2]):
        for cp in range(C):
            arrived(wb.at[:, rows, cols], wr.at[i * C + cp])
        shard = pl.ds(pl.multiple_of(lax.rem(yl + YL - hop % YL, YL) * C * RT, C * RT), C * RT)
        where = dev(lax.rem(y + hop, Y), z, x, c)
        sends.append(send(wb.at[:, shard, cols], wb.at[:, shard, cols], ws.at[9 + i], wr.at[9 + i], where))

    pairs = [(1, 1), (1, 0), (0, 1), (0, 0)]
    for i, (hop, cols) in enumerate(routes[2:]):
        for cp in range(C):
            arrived(wb.at[:, rows, cols], wr.at[(2 + i) * C + cp])
    arrived(wb.at[:, rows, :], wr.at[8])
    for i, (hop, cols) in enumerate(routes[:2]):
        shard = pl.ds(0, C * RT)
        arrived(wb.at[:, shard, cols], wr.at[9 + i])
    for ex, ez in pairs:
        for ec in range(C):
            if ex or ez or ec:
                arrived(bx.at[me], xr.at[number(ex, ez, ec)])
        g = across(px, ex) * 2 + across(pz, ez)
        a = bx[pl.ds(g * C, C)].reshape(C * TOK, CC)
        gate_up = lax.dot_general(a, wb[0:2].reshape(2 * HID, CC), NT, preferred_element_type=jnp.float32)
        for cc in range(C):
            part = slice(cc * TOK, (cc + 1) * TOK)
            pt[g * C + cc, 0:TOK] = gate_up[part, :HID]
            pt[g * C + cc, TOK:] = gate_up[part, HID:]
        for ec in range(C):
            if ex or ez or ec:
                n, core = number(ex, ez, ec), across(c, ec)
                sends.append(send(pt.at[g * C + core], rx.at[me], ps.at[n], pr.at[n], even(ex, ez, core)))
    for ex, ez in pairs:
        for ec in range(C):
            if ex or ez or ec:
                arrived(bd.at[me], dr.at[number(ex, ez, ec)])
        g = across(px, ex) * 2 + across(pz, ez)
        d = bd[pl.ds(g * C, C)].reshape(C * TOK, CC)
        dh = lax.dot_general(d, wb[2], NT, preferred_element_type=jnp.float32)
        for cc in range(C):
            pd[g * C + cc] = dh[cc * TOK : (cc + 1) * TOK]
        for ec in range(C):
            if ex or ez or ec:
                n, core = number(ex, ez, ec), across(c, ec)
                sends.append(send(pd.at[g * C + core], rd.at[me], qs.at[n], qr.at[n], odd(ex, ez, core)))
    for n in range(3):
        arrived(n1.at[square], n1r.at[n])
    m2[kme] = added(n1, 4)
    for rel in range(1, BLOCKS):
        k = lax.rem(kme + rel, BLOCKS)
        sends.append(send(m2.at[kme], m2.at[kme], n2s.at[rel], n2r.at[kme], class_dev(k)))
    rx[me] = pt[me]
    rd[me] = pd[me]
    for n in range(1, SLOTS):
        arrived(rx.at[me], pr.at[n])
    total = rx[0]
    for n in range(1, SLOTS):
        total = total + rx[n]
    gate, up = total[:TOK], total[TOK:]
    sig = 1.0 / (1.0 + jnp.exp(-gate))
    silu = gate * sig
    first = lax.broadcasted_iota(jnp.int32, (TOK, HID), 0) < RT
    keep_rows = jnp.where(first, 1 - ovf[0, 0], 1 - ovf[0, 1]) > 0
    zero = jnp.zeros((TOK, HID), jnp.float32)
    hb[me] = jnp.where(keep_rows, silu * up, zero).astype(jnp.bfloat16)
    for ex, ez, ec in others:
        n = number(ex, ez, ec)
        sends.append(send(hb.at[me], hb.at[me], hs.at[n], hr.at[n], odd(ex, ez, across(c, ec))))
    for n in range(1, SLOTS):
        arrived(rd.at[me], qr.at[n])
    dh = rd[0]
    for n in range(1, SLOTS):
        dh = dh + rd[n]
    ab[me, 0] = jnp.where(keep_rows, dh * up * sig * (1.0 + gate * (1.0 - sig)), zero).astype(jnp.bfloat16)
    ab[me, 1] = jnp.where(keep_rows, dh * silu, zero).astype(jnp.bfloat16)
    for ex, ez, ec in others:
        n = number(ex, ez, ec)
        sends.append(send(ab.at[me], ab.at[me], as_.at[n], ar.at[n], even(ex, ez, across(c, ec))))
    from_z(m2, n2r)
    m3[yh] = added(m2, BLOCKS)
    sends.append(send(m3.at[yh], m3.at[yh], n3s, n3r, dev(lax.rem(y + YL, Y), z, x, c)))
    for n in range(1, SLOTS):
        arrived(hb.at[me], hr.at[n])
        arrived(ab.at[me], ar.at[n])

    lhs = [jnp.transpose(v.reshape(SLOTS * TOK, HID)) for v in (ab[:, 0], ab[:, 1], hb[...])]
    lhs_gu = jnp.concatenate(lhs[:2], axis=0)
    wide = 2 * LANES
    for zt in range(BLOCKS // 2):
        cols = slice(zt * wide, (zt + 1) * wide)
        acts_cols = bx[:, :, :, cols].reshape(SLOTS * TOK, wide)
        dy_cols = bd[:, :, :, cols].reshape(SLOTS * TOK, wide)
        gu = jnp.dot(lhs_gu, acts_cols, preferred_element_type=jnp.float32)
        dn = jnp.dot(lhs[2], dy_cols, preferred_element_type=jnp.float32)
        for k, block in enumerate([gu[:HID], gu[HID:], dn]):
            pair = [block[:, :LANES], block[:, LANES:]]
            for b in range(2):
                low = [pair[b][i * RT : i * RT + 8] for i in range(YL * C)]
                sz[zt * 2 + b, k * 64 : (k + 1) * 64] = jnp.concatenate(low, axis=0).astype(jnp.bfloat16)
            for i in range(YL * C):
                high = [p[i * RT + 8 : (i + 1) * RT] for p in pair]
                at = k * 8 * BLOCKS + zt * 16
                sy[i, at : at + 16] = jnp.concatenate(high, axis=0).astype(jnp.bfloat16)

    to_y(sy, ry, ys, yr)
    to_z(sz, rz, zs, zr)
    from_y(sy, ry, ys, yr)
    high = added(ry, Y)
    for k in range(BLOCKS):
        for m in range(3):
            at = m * 8 * BLOCKS + k * 8
            s2z[k, m * 8 : (m + 1) * 8] = high[at : at + 8]
    to_z(s2z, r2z, z2s, z2r)
    from_z(rz, zr)
    low = added(rz, BLOCKS)
    for i in range(YL * C):
        for m in range(3):
            s2y[i, m * 8 : (m + 1) * 8] = low[m * 64 + i * 8 : m * 64 + (i + 1) * 8]
    to_y(s2y, r2y, y2s, y2r)
    from_z(r2z, z2r)
    high = added(r2z, BLOCKS)
    from_y(s2y, r2y, y2s, y2r)
    low = added(r2y, Y)
    arrived(m3.at[yh], n3r)
    n_dp = lax.axis_size("dp")
    count = m3[0] + m3[1]
    rate = 0.01 * (1.0 - count / jnp.float32(MB * n_dp))
    for m in range(3):
        out[m, 0:8] = low[m * 8 : (m + 1) * 8] / jnp.float32(MB * n_dp)
        out[m, 8:16] = high[m * 8 : (m + 1) * 8] / jnp.float32(MB * n_dp)
        rate_out[m, 0:8] = rate
        rate_out[m, 8:16] = rate

    for copy in sends:
        copy.wait_send()


def per_device(acts, grad_out, w_gate, w_up, w_down, overflow, step, master, moment1, moment2):
    d = acts.shape[2]
    bf16, f32 = jnp.bfloat16, jnp.float32
    dma = pltpu.SemaphoreType.DMA
    grad, rate = pl.pallas_call(
        kernel,
        out_shape=(jax.ShapeDtypeStruct((3, RT, LANES), f32),) * 2,
        in_specs=[pl.BlockSpec(memory_space=pl.ANY)] * 6,
        out_specs=(pl.BlockSpec(memory_space=pltpu.VMEM),) * 2,
        scratch_shapes=[
            pltpu.SMEM((1, MB), jnp.int32),
            pltpu.VMEM((MB, RT, d), bf16),
            pltpu.VMEM((MB, RT, d), bf16),
            pltpu.VMEM((3, RT, d), bf16),
            pltpu.VMEM((SLOTS, MB, RT, CC), bf16),
            pltpu.VMEM((SLOTS, MB, RT, CC), bf16),
            pltpu.VMEM((SLOTS, MB, RT, CC), bf16),
            pltpu.VMEM((SLOTS, MB, RT, CC), bf16),
            pltpu.VMEM((C, 3, RT, CC), bf16),
            pltpu.VMEM((3, HID, CC), bf16),
            pltpu.VMEM((SLOTS, 2 * TOK, LANES), f32),
            pltpu.VMEM((SLOTS, TOK, LANES), f32),
            pltpu.VMEM((SLOTS, 2 * TOK, LANES), f32),
            pltpu.VMEM((SLOTS, TOK, LANES), f32),
            pltpu.VMEM((SLOTS, 2, TOK, HID), bf16),
            pltpu.VMEM((SLOTS, TOK, HID), bf16),
            pltpu.VMEM((BLOCKS, 192, LANES), bf16),
            pltpu.VMEM((BLOCKS, 192, LANES), bf16),
            pltpu.VMEM((YL * C, 24 * BLOCKS, LANES), bf16),
            pltpu.VMEM((Y, 24 * BLOCKS, LANES), bf16),
            pltpu.VMEM((YL * C, 24, LANES), f32),
            pltpu.VMEM((Y, 24, LANES), f32),
            pltpu.VMEM((BLOCKS, 24, LANES), f32),
            pltpu.VMEM((BLOCKS, 24, LANES), f32),
            pltpu.VMEM((4, 8, LANES), f32),
            pltpu.VMEM((BLOCKS, 8, LANES), f32),
            pltpu.VMEM((YH, 8, LANES), f32),
            dma((6,)),
            dma((SLOTS,)), dma((SLOTS,)),
            dma((SLOTS,)), dma((SLOTS,)),
            dma((11,)), dma((11,)),
            dma((SLOTS,)), dma((SLOTS,)),
            dma((SLOTS,)), dma((SLOTS,)),
            dma((SLOTS,)), dma((SLOTS,)),
            dma((SLOTS,)), dma((SLOTS,)),
            dma((BLOCKS,)), dma((BLOCKS,)),
            dma((Y,)), dma((Y,)),
            dma((Y,)), dma((Y,)),
            dma((BLOCKS,)), dma((BLOCKS,)),
            dma((3,)), dma((3,)),
            dma((BLOCKS,)), dma((BLOCKS,)),
            dma, dma,
        ],
        compiler_params=pltpu.CompilerParams(
            collective_id=0, has_side_effects=True, vmem_limit_bytes=63 * 1024 * 1024
        ),
        name="window_grads",
    )(acts, grad_out, w_gate.T, w_up.T, w_down, overflow)
    new_moment1 = 0.9 * moment1 + 0.1 * grad
    new_moment2 = 0.95 * moment2 + 0.05 * grad * grad
    steps_f = step[0].astype(f32)
    corr1 = 1.0 - jnp.power(f32(0.9), steps_f)
    corr2 = 1.0 - jnp.power(f32(0.95), steps_f)
    direction = new_moment1 / corr1 / (jnp.sqrt(new_moment2 / corr2) + 1e-08)
    new_master = master - rate * (direction + 0.1 * master)
    return (new_master, new_moment1, new_moment2)


def solution(mesh):
    in_specs = (
        P(None, ("dp", "tensor"), None),
        P(None, ("dp", "tensor"), None),
        P(None, "tensor"),
        P(None, "tensor"),
        P("tensor", None),
        P("dp", None),
        P(),
        P(None, "tensor", "dp"),
        P(None, "tensor", "dp"),
        P(None, "tensor", "dp"),
    )
    out_specs = (P(None, "tensor", "dp"), P(None, "tensor", "dp"), P(None, "tensor", "dp"))
    return jax.shard_map(
        per_device, mesh=mesh, in_specs=in_specs, out_specs=out_specs, check_vma=False
    )
```

time: 1030 us -> 61.4 us (0.06)
  waiting for transfers between devices: 961 us -> 0 us
  Pallas kernels: 0 us -> 58.3 us
  blocking collectives: 22 us -> 0 us
  matrix products: 15 us -> 0 us
  between operations: 15.2 us -> 1.42 us
    reduce_scatter x1 -> x0, waiting for transfers between devices: 798 us -> none  [per_device(): summed = lax.psum_scatter(total, 'dp', scatter_dimension=2, tiled=True)]
    all_gather x4 -> x0, waiting for transfers between devices: 161 us -> none  [the longest x2 81.3 us: per_device(): lax.all_gather(acts[index], 'tensor', axis=0, tiled=True)]
    pallas_call x0 -> x1, Pallas kernels: none -> 58.3 us  [per_device(): pl.pallas_call(kernel, out_shape=(jax.ShapeDtypeStruct((3, RT, LANES), f3...]
    psum x1 -> x0, blocking collectives: 22 us -> none  [per_device(): count = lax.psum(local_count, 'dp').astype(jnp.float32)]
    dot_general x12 -> x0, matrix products: 15 us -> none  [the longest x6 4.97 us: contract_rows(): lax.dot_general(left, right, (((0,), (0,)), ((), ())), preferred_element_...]
  transfers between devices with their start and end apart: 5 -> 0, of which waited for: 5 -> 0; matrix products, arithmetic and copies ran while one was open for 1% -> 0% of each run, Pallas kernels for 0% -> 0%
where the time goes in v2:
time: 61.4 us; the launch traced here: 61.1 us
  Pallas kernels  58.3 us (95%)
  between operations  1.42 us (2%)
  other arithmetic  1.4 us (2%)
    pallas_call x1, Pallas kernels, per_device(): pl.pallas_call(kernel, out_shape=(jax.ShapeDtypeStruct((3, RT, LANES), f3...  58.3 us
    sub x1, other arithmetic, per_device(): new_master = master - rate * (direction + 0.1 * master)  1.4 us

profile of v2, /device:TPU:1, one launch (start us, length us, event | category | flops | bytes accessed | tf_op | source)
XLA Modules:
  0.0 61.1 jit_solution(8147789084842869997)
XLA Ops:
  1.4 0.0 copy-start
  1.4 0.0 copy-start.1
  1.4 0.0 copy-start.2
  1.4 58.3 %window_grads.1 = (f32[3,16,128]{2,1,0:T(8,128)}, f32[3,16,128]{2,1,0:T(8,128)}) custom-call(bf16[2,16,8192]{2,1,0:T(8,128)(2,1)} %acts_hbm.1, bf16[2,16,8192]{2,1,0:T(8,128)(2,1)} %dy_hbm.1, bf16[16,8192]{1,0:T(8,128)(2,1)} %bitcast.4, bf16[16,8192]{1,0:T(8,128)(2,1)} %bitcast.5, bf16[16,8192]{1,0:T(8,128)(2,1)} %wd_hbm.1, s32[1,2]{1,0:T(1,128)} %ovf_hbm.1), custom_call_target="tpu_custom_call" | custom-call | tf_op jit(solution)/shard_map/window_grads/pallas_call | solution.py:329
  59.7 0.0 copy-done
  59.7 0.0 copy-done.1
  59.7 0.0 copy-done.2
  59.7 1.4 %multiply_subtract_fusion = (f32[3,16,128]{2,1,0:T(8,128)}, f32[3,16,128]{2,1,0:T(8,128)}, f32[3,16,128]{2,1,0:T(8,128)}) fusion(f32[3,16,128]{2,1,0:T(8,128)S(1)} %copy-done, f32[3,16,128]{2,1,0:T(8,128)} %get-tuple-element.5, f32[]{:T(128)} %bitcast.3, f32[]{:T(128)} %bitcast.2, f32[3,16,128]{2,1,0:T(8,128)} %get-tuple-element.6, ...), kind=kLoop, calls=%fused_computation.2 | loop fusion | flops 92160 | bytes 196616 | tf_op jit(solution)/shard_map/sub | solution.py:389
Async XLA Ops:
  1.4 58.3 %copy-start = (f32[3,16,128]{2,1,0:T(8,128)S(1)}, f32[3,16,128]{2,1,0:T(8,128)}, u32[]{:S(2)}) copy-start(f32[3,16,128]{2,1,0:T(8,128)} %param.17) | copy-start | bytes 73732
  1.4 58.3 %copy-start.1 = (f32[3,16,128]{2,1,0:T(8,128)S(1)}, f32[3,16,128]{2,1,0:T(8,128)}, u32[]{:S(2)}) copy-start(f32[3,16,128]{2,1,0:T(8,128)} %param.19) | copy-start | bytes 73732
  1.4 58.3 %copy-start.2 = (f32[3,16,128]{2,1,0:T(8,128)S(1)}, f32[3,16,128]{2,1,0:T(8,128)}, u32[]{:S(2)}) copy-start(f32[3,16,128]{2,1,0:T(8,128)} %param.18) | copy-start | bytes 73732

commit v3 on v2

--- a/solution.py
+++ b/solution.py
@@ -15,6 +15,7 @@
 BLOCKS = (X // 2) * (Z // 2)
 CC = BLOCKS * LANES
 HID = 128
+LOW = (8, 8, 8)
 MESH = pl.DeviceIdType.MESH
 NT = (((1,), (1,)), ((), ()))
 
@@ -87,8 +88,6 @@
     def class_dev(k):
         return dev(y, lax.div(k, X // 2) * 2 + pz, lax.rem(k, X // 2) * 2 + px, c)
 
-    for step in range(1, BLOCKS):
-        friends.append(class_dev(lax.rem(kme + step, BLOCKS)))
     for friend in friends:
         pl.semaphore_signal(barrier, inc=1, device_id=friend, device_id_type=MESH)
 
@@ -177,10 +176,8 @@
         sends.append(send(sx.at[n], bx.at[me], xs.at[n], xr.at[n], even(ex, ez, across(c, ec))))
         sends.append(send(sd.at[n], bd.at[me], ds.at[n], dr.at[n], odd(ex, ez, across(c, ec))))
     lost = (ovf[0, 0] + ovf[0, 1]).astype(jnp.float32)
-    square = px * 2 + pz
-    n1[square] = jnp.full((8, LANES), lost, jnp.float32)
-    for n, (ex, ez) in enumerate([(1, 1), (1, 0), (0, 1)]):
-        sends.append(send(n1.at[square], n1.at[square], n1s.at[n], n1r.at[n], even(ex, ez, c)))
+    m3[yh] = jnp.full((8, LANES), lost, jnp.float32)
+    sends.append(send(m3.at[yh], m3.at[yh], n3s, n3r, dev(lax.rem(y + YL, Y), z, x, c)))
     wb[:, rows, :] = sw[c]
     for k in range(BLOCKS):
         at = columns(k, px, pz, c)
@@ -193,6 +190,12 @@
         shard = pl.ds(pl.multiple_of(lax.rem(yl + YL - hop % YL, YL) * C * RT, C * RT), C * RT)
         where = dev(lax.rem(y + hop, Y), z, x, c)
         sends.append(send(wb.at[:, shard, cols], wb.at[:, shard, cols], ws.at[9 + i], wr.at[9 + i], where))
+
+    square = px * 2 + pz
+    arrived(m3.at[yh], n3r)
+    n1[square] = m3[0] + m3[1]
+    for n, (ex, ez) in enumerate([(1, 1), (1, 0), (0, 1)]):
+        sends.append(send(n1.at[square], n1.at[square], n1s.at[n], n1r.at[n], even(ex, ez, c)))
 
     pairs = [(1, 1), (1, 0), (0, 1), (0, 0)]
     for i, (hop, cols) in enumerate(routes[2:]):
@@ -230,12 +233,6 @@
             if ex or ez or ec:
                 n, core = number(ex, ez, ec), across(c, ec)
                 sends.append(send(pd.at[g * C + core], rd.at[me], qs.at[n], qr.at[n], odd(ex, ez, core)))
-    for n in range(3):
-        arrived(n1.at[square], n1r.at[n])
-    m2[kme] = added(n1, 4)
-    for rel in range(1, BLOCKS):
-        k = lax.rem(kme + rel, BLOCKS)
-        sends.append(send(m2.at[kme], m2.at[kme], n2s.at[rel], n2r.at[kme], class_dev(k)))
     rx[me] = pt[me]
     rd[me] = pd[me]
     for n in range(1, SLOTS):
@@ -263,9 +260,6 @@
     for ex, ez, ec in others:
         n = number(ex, ez, ec)
         sends.append(send(ab.at[me], ab.at[me], as_.at[n], ar.at[n], even(ex, ez, across(c, ec))))
-    from_z(m2, n2r)
-    m3[yh] = added(m2, BLOCKS)
-    sends.append(send(m3.at[yh], m3.at[yh], n3s, n3r, dev(lax.rem(y + YL, Y), z, x, c)))
     for n in range(1, SLOTS):
         arrived(hb.at[me], hr.at[n])
         arrived(ab.at[me], ar.at[n])
@@ -281,40 +275,55 @@
         dn = jnp.dot(lhs[2], dy_cols, preferred_element_type=jnp.float32)
         for k, block in enumerate([gu[:HID], gu[HID:], dn]):
             pair = [block[:, :LANES], block[:, LANES:]]
+            n_low, n_high = LOW[k], RT - LOW[k]
             for b in range(2):
-                low = [pair[b][i * RT : i * RT + 8] for i in range(YL * C)]
-                sz[zt * 2 + b, k * 64 : (k + 1) * 64] = jnp.concatenate(low, axis=0).astype(jnp.bfloat16)
-            for i in range(YL * C):
-                high = [p[i * RT + 8 : (i + 1) * RT] for p in pair]
-                at = k * 8 * BLOCKS + zt * 16
-                sy[i, at : at + 16] = jnp.concatenate(high, axis=0).astype(jnp.bfloat16)
+                low = [pair[b][i * RT : i * RT + n_low] for i in range(YL * C)]
+                at = sum(LOW[:k]) * YL * C
+                sz[zt * 2 + b, at : at + n_low * YL * C] = jnp.concatenate(low, axis=0).astype(jnp.bfloat16)
+            for i in range(YL * C if n_high else 0):
+                high = [p[i * RT + n_low : (i + 1) * RT] for p in pair]
+                at = (k * RT - sum(LOW[:k])) * BLOCKS + zt * 2 * n_high
+                sy[i, at : at + 2 * n_high] = jnp.concatenate(high, axis=0).astype(jnp.bfloat16)
 
     to_y(sy, ry, ys, yr)
     to_z(sz, rz, zs, zr)
+    for n in range(3):
+        arrived(n1.at[square], n1r.at[n])
+    m2[kme] = added(n1, 4)
+    for rel in range(1, BLOCKS):
+        k = lax.rem(kme + rel, BLOCKS)
+        sends.append(send(m2.at[kme], m2.at[kme], n2s.at[rel], n2r.at[kme], class_dev(k)))
     from_y(sy, ry, ys, yr)
     high = added(ry, Y)
     for k in range(BLOCKS):
         for m in range(3):
-            at = m * 8 * BLOCKS + k * 8
-            s2z[k, m * 8 : (m + 1) * 8] = high[at : at + 8]
+            n_high, to = RT - LOW[m], m * RT - sum(LOW[:m])
+            if n_high:
+                at = to * BLOCKS + k * n_high
+                s2z[k, to : to + n_high] = high[at : at + n_high]
     to_z(s2z, r2z, z2s, z2r)
     from_z(rz, zr)
     low = added(rz, BLOCKS)
     for i in range(YL * C):
         for m in range(3):
-            s2y[i, m * 8 : (m + 1) * 8] = low[m * 64 + i * 8 : m * 64 + (i + 1) * 8]
+            n_low, to = LOW[m], sum(LOW[:m])
+            at = to * YL * C + i * n_low
+            s2y[i, to : to + n_low] = low[at : at + n_low]
     to_y(s2y, r2y, y2s, y2r)
     from_z(r2z, z2r)
     high = added(r2z, BLOCKS)
     from_y(s2y, r2y, y2s, y2r)
     low = added(r2y, Y)
-    arrived(m3.at[yh], n3r)
+    from_z(m2, n2r)
     n_dp = lax.axis_size("dp")
-    count = m3[0] + m3[1]
+    count = added(m2, BLOCKS)
     rate = 0.01 * (1.0 - count / jnp.float32(MB * n_dp))
     for m in range(3):
-        out[m, 0:8] = low[m * 8 : (m + 1) * 8] / jnp.float32(MB * n_dp)
-        out[m, 8:16] = high[m * 8 : (m + 1) * 8] / jnp.float32(MB * n_dp)
+        n_low, at = LOW[m], sum(LOW[:m])
+        out[m, 0:n_low] = low[at : at + n_low] / jnp.float32(MB * n_dp)
+        if n_low < RT:
+            at = m * RT - at
+            out[m, n_low:RT] = high[at : at + RT - n_low] / jnp.float32(MB * n_dp)
         rate_out[m, 0:8] = rate
         rate_out[m, 8:16] = rate
 
@@ -348,14 +357,14 @@
             pltpu.VMEM((SLOTS, TOK, LANES), f32),
             pltpu.VMEM((SLOTS, 2, TOK, HID), bf16),
             pltpu.VMEM((SLOTS, TOK, HID), bf16),
-            pltpu.VMEM((BLOCKS, 192, LANES), bf16),
-            pltpu.VMEM((BLOCKS, 192, LANES), bf16),
-            pltpu.VMEM((YL * C, 24 * BLOCKS, LANES), bf16),
-            pltpu.VMEM((Y, 24 * BLOCKS, LANES), bf16),
-            pltpu.VMEM((YL * C, 24, LANES), f32),
-            pltpu.VMEM((Y, 24, LANES), f32),
-            pltpu.VMEM((BLOCKS, 24, LANES), f32),
-            pltpu.VMEM((BLOCKS, 24, LANES), f32),
+            pltpu.VMEM((BLOCKS, sum(LOW) * YL * C, LANES), bf16),
+            pltpu.VMEM((BLOCKS, sum(LOW) * YL * C, LANES), bf16),
+            pltpu.VMEM((YL * C, (3 * RT - sum(LOW)) * BLOCKS, LANES), bf16),
+            pltpu.VMEM((Y, (3 * RT - sum(LOW)) * BLOCKS, LANES), bf16),
+            pltpu.VMEM((YL * C, sum(LOW), LANES), f32),
+            pltpu.VMEM((Y, sum(LOW), LANES), f32),
+            pltpu.VMEM((BLOCKS, 3 * RT - sum(LOW), LANES), f32),
+            pltpu.VMEM((BLOCKS, 3 * RT - sum(LOW), LANES), f32),
             pltpu.VMEM((4, 8, LANES), f32),
             pltpu.VMEM((BLOCKS, 8, LANES), f32),
             pltpu.VMEM((YH, 8, LANES), f32),

time: 61.4 us -> 57.9 us (0.943)
  Pallas kernels: 58.3 us -> 54.8 us
    pallas_call x1, Pallas kernels: 58.3 us -> 54.8 us  [per_device(): pl.pallas_call(kernel, out_shape=(jax.ShapeDtypeStruct((3, RT, LANES), f3...]
where the time goes in v3:
time: 57.9 us; the launch traced here: 57.7 us
  Pallas kernels  54.8 us (95%)
  between operations  1.42 us (2%)
  other arithmetic  1.4 us (2%)
    pallas_call x1, Pallas kernels, per_device(): pl.pallas_call(kernel, out_shape=(jax.ShapeDtypeStruct((3, RT, LANES), f3...  54.8 us
    sub x1, other arithmetic, per_device(): new_master = master - rate * (direction + 0.1 * master)  1.4 us

profile of v3, /device:TPU:1, one launch (start us, length us, event | category | flops | bytes accessed | tf_op | source)
XLA Modules:
  0.0 57.7 jit_solution(17219338531729684037)
XLA Ops:
  1.4 0.0 copy-start
  1.4 0.0 copy-start.1
  1.4 0.0 copy-start.2
  1.4 54.8 %window_grads.1 = (f32[3,16,128]{2,1,0:T(8,128)}, f32[3,16,128]{2,1,0:T(8,128)}) custom-call(bf16[2,16,8192]{2,1,0:T(8,128)(2,1)} %acts_hbm.1, bf16[2,16,8192]{2,1,0:T(8,128)(2,1)} %dy_hbm.1, bf16[16,8192]{1,0:T(8,128)(2,1)} %bitcast.4, bf16[16,8192]{1,0:T(8,128)(2,1)} %bitcast.5, bf16[16,8192]{1,0:T(8,128)(2,1)} %wd_hbm.1, s32[1,2]{1,0:T(1,128)} %ovf_hbm.1), custom_call_target="tpu_custom_call" | custom-call | tf_op jit(solution)/shard_map/window_grads/pallas_call | solution.py:338
  56.2 0.0 copy-done
  56.2 0.0 copy-done.1
  56.2 0.0 copy-done.2
  56.3 1.4 %multiply_subtract_fusion = (f32[3,16,128]{2,1,0:T(8,128)}, f32[3,16,128]{2,1,0:T(8,128)}, f32[3,16,128]{2,1,0:T(8,128)}) fusion(f32[3,16,128]{2,1,0:T(8,128)S(1)} %copy-done, f32[3,16,128]{2,1,0:T(8,128)} %get-tuple-element.5, f32[]{:T(128)} %bitcast.3, f32[]{:T(128)} %bitcast.2, f32[3,16,128]{2,1,0:T(8,128)} %get-tuple-element.6, ...), kind=kLoop, calls=%fused_computation.2 | loop fusion | flops 92160 | bytes 196616 | tf_op jit(solution)/shard_map/sub | solution.py:398
Async XLA Ops:
  1.4 54.9 %copy-start = (f32[3,16,128]{2,1,0:T(8,128)S(1)}, f32[3,16,128]{2,1,0:T(8,128)}, u32[]{:S(2)}) copy-start(f32[3,16,128]{2,1,0:T(8,128)} %param.17) | copy-start | bytes 73732
  1.4 54.9 %copy-start.1 = (f32[3,16,128]{2,1,0:T(8,128)S(1)}, f32[3,16,128]{2,1,0:T(8,128)}, u32[]{:S(2)}) copy-start(f32[3,16,128]{2,1,0:T(8,128)} %param.19) | copy-start | bytes 73732
  1.4 54.9 %copy-start.2 = (f32[3,16,128]{2,1,0:T(8,128)S(1)}, f32[3,16,128]{2,1,0:T(8,128)}, u32[]{:S(2)}) copy-start(f32[3,16,128]{2,1,0:T(8,128)} %param.18) | copy-start | bytes 73732

commit v4 on v3

--- a/solution.py
+++ b/solution.py
@@ -15,7 +15,7 @@
 BLOCKS = (X // 2) * (Z // 2)
 CC = BLOCKS * LANES
 HID = 128
-LOW = (8, 8, 8)
+LOW = 8
 MESH = pl.DeviceIdType.MESH
 NT = (((1,), (1,)), ((), ()))
 
@@ -26,8 +26,8 @@
 
 def kernel(
     acts_hbm, dy_hbm, wg_hbm, wu_hbm, wd_hbm, ovf_hbm, out, rate_out,
-    ovf, acts_v, dy_v, w_v, sx, sd, bx, bd, sw, wb, pt, pd, rx, rd, ab, hb, sz, rz, sy, ry, s2y, r2y, s2z, r2z,
-    n1, m2, m3, ld, xs, xr, ds, dr, ws, wr, ps, pr, qs, qr, as_, ar, hs, hr, zs, zr, ys, yr, y2s, y2r, z2s, z2r,
+    ovf, acts_v, dy_v, w_v, sx, sd, bx, bd, sw, wb, pt, pd, rx, rd, ab, hb, sz, rz, sy, ry, szd, rzd, syd, ryd, s2y, r2y, s2z, r2z,
+    n1, m2, m3, ld, xs, xr, ds, dr, ws, wr, ps, pr, qs, qr, as_, ar, hs, hr, zs, zr, ys, yr, zds, zdr, yds, ydr, y2s, y2r, z2s, z2r,
     n1s, n1r, n2s, n2r, n3s, n3r,
 ):
     dp, t = lax.axis_index("dp"), lax.axis_index("tensor")
@@ -140,11 +140,13 @@
             arrived(slots.at[y], recv_sems.at[y])
             pltpu.make_async_copy(buf.at[t], buf.at[t], send_sems.at[0]).wait()
 
-    def to_z(buf, slots, send_sems, recv_sems):
-        for rel in range(1, BLOCKS):
-            k = lax.rem(kme + rel, BLOCKS)
-            sends.append(send(buf.at[k], slots.at[kme], send_sems.at[rel], recv_sems.at[kme], class_dev(k)))
-        slots[kme] = buf[kme]
+    near = [(0, 1), (1, 0), (1, 1), (3, 0), (3, 1)]
+    far = [(2, 0), (2, 1)]
+
+    def to_z(buf, slots, send_sems, recv_sems, steps):
+        for kz, kx in steps:
+            k = lax.rem(lax.div(z, 2) + kz, Z // 2) * 2 + across(lax.div(x, 2), kx)
+            sends.append(send(buf.at[k], slots.at[kme], send_sems.at[kz * 2 + kx], recv_sems.at[kme], class_dev(k)))
 
     def from_z(slots, recv_sems):
         for rel in range(1, BLOCKS):
@@ -260,55 +262,60 @@
     for ex, ez, ec in others:
         n = number(ex, ez, ec)
         sends.append(send(ab.at[me], ab.at[me], as_.at[n], ar.at[n], even(ex, ez, across(c, ec))))
+    def products(lhs, tokens, low_buf, high_buf):
+        wide = 2 * LANES
+        for zt in range(BLOCKS // 2):
+            cols = slice(zt * wide, (zt + 1) * wide)
+            rhs = tokens[:, :, :, cols].reshape(SLOTS * TOK, wide)
+            summed = jnp.dot(lhs, rhs, preferred_element_type=jnp.float32)
+            for k in range(lhs.shape[0] // HID):
+                block = summed[k * HID : (k + 1) * HID]
+                pair = [block[:, :LANES], block[:, LANES:]]
+                at = k * LOW * YL * C
+                for b in range(2):
+                    low = [pair[b][i * RT : i * RT + LOW] for i in range(YL * C)]
+                    low_buf[zt * 2 + b, at : at + LOW * YL * C] = jnp.concatenate(low, axis=0).astype(jnp.bfloat16)
+                at = k * 8 * BLOCKS + zt * 16
+                for i in range(YL * C):
+                    high = [p[i * RT + LOW : (i + 1) * RT] for p in pair]
+                    high_buf[i, at : at + 16] = jnp.concatenate(high, axis=0).astype(jnp.bfloat16)
+
     for n in range(1, SLOTS):
         arrived(hb.at[me], hr.at[n])
+    products(jnp.transpose(hb[...].reshape(SLOTS * TOK, HID)), bd, szd, syd)
+    to_y(syd, ryd, yds, ydr)
+    to_z(szd, rzd, zds, zdr, near)
+    for n in range(1, SLOTS):
         arrived(ab.at[me], ar.at[n])
-
-    lhs = [jnp.transpose(v.reshape(SLOTS * TOK, HID)) for v in (ab[:, 0], ab[:, 1], hb[...])]
-    lhs_gu = jnp.concatenate(lhs[:2], axis=0)
-    wide = 2 * LANES
-    for zt in range(BLOCKS // 2):
-        cols = slice(zt * wide, (zt + 1) * wide)
-        acts_cols = bx[:, :, :, cols].reshape(SLOTS * TOK, wide)
-        dy_cols = bd[:, :, :, cols].reshape(SLOTS * TOK, wide)
-        gu = jnp.dot(lhs_gu, acts_cols, preferred_element_type=jnp.float32)
-        dn = jnp.dot(lhs[2], dy_cols, preferred_element_type=jnp.float32)
-        for k, block in enumerate([gu[:HID], gu[HID:], dn]):
-            pair = [block[:, :LANES], block[:, LANES:]]
-            n_low, n_high = LOW[k], RT - LOW[k]
-            for b in range(2):
-                low = [pair[b][i * RT : i * RT + n_low] for i in range(YL * C)]
-                at = sum(LOW[:k]) * YL * C
-                sz[zt * 2 + b, at : at + n_low * YL * C] = jnp.concatenate(low, axis=0).astype(jnp.bfloat16)
-            for i in range(YL * C if n_high else 0):
-                high = [p[i * RT + n_low : (i + 1) * RT] for p in pair]
-                at = (k * RT - sum(LOW[:k])) * BLOCKS + zt * 2 * n_high
-                sy[i, at : at + 2 * n_high] = jnp.concatenate(high, axis=0).astype(jnp.bfloat16)
-
+    to_z(szd, rzd, zds, zdr, far)
+    rzd[kme] = szd[kme]
+    lhs = [jnp.transpose(ab[:, k].reshape(SLOTS * TOK, HID)) for k in range(2)]
+    products(jnp.concatenate(lhs, axis=0), bx, sz, sy)
     to_y(sy, ry, ys, yr)
-    to_z(sz, rz, zs, zr)
+    to_z(sz, rz, zs, zr, near + far)
+    rz[kme] = sz[kme]
     for n in range(3):
         arrived(n1.at[square], n1r.at[n])
     m2[kme] = added(n1, 4)
     for rel in range(1, BLOCKS):
         k = lax.rem(kme + rel, BLOCKS)
         sends.append(send(m2.at[kme], m2.at[kme], n2s.at[rel], n2r.at[kme], class_dev(k)))
+    from_y(syd, ryd, yds, ydr)
     from_y(sy, ry, ys, yr)
-    high = added(ry, Y)
+    high = (added(ry, Y), added(ryd, Y))
     for k in range(BLOCKS):
         for m in range(3):
-            n_high, to = RT - LOW[m], m * RT - sum(LOW[:m])
-            if n_high:
-                at = to * BLOCKS + k * n_high
-                s2z[k, to : to + n_high] = high[at : at + n_high]
-    to_z(s2z, r2z, z2s, z2r)
+            at = m % 2 * 8 * BLOCKS + k * 8
+            s2z[k, m * 8 : (m + 1) * 8] = high[m // 2][at : at + 8]
+    to_z(s2z, r2z, z2s, z2r, near + far)
+    r2z[kme] = s2z[kme]
+    from_z(rzd, zdr)
     from_z(rz, zr)
-    low = added(rz, BLOCKS)
+    low = (added(rz, BLOCKS), added(rzd, BLOCKS))
     for i in range(YL * C):
         for m in range(3):
-            n_low, to = LOW[m], sum(LOW[:m])
-            at = to * YL * C + i * n_low
-            s2y[i, to : to + n_low] = low[at : at + n_low]
+            at = m % 2 * LOW * YL * C + i * LOW
+            s2y[i, m * LOW : (m + 1) * LOW] = low[m // 2][at : at + LOW]
     to_y(s2y, r2y, y2s, y2r)
     from_z(r2z, z2r)
     high = added(r2z, BLOCKS)
@@ -319,11 +326,8 @@
     count = added(m2, BLOCKS)
     rate = 0.01 * (1.0 - count / jnp.float32(MB * n_dp))
     for m in range(3):
-        n_low, at = LOW[m], sum(LOW[:m])
-        out[m, 0:n_low] = low[at : at + n_low] / jnp.float32(MB * n_dp)
-        if n_low < RT:
-            at = m * RT - at
-            out[m, n_low:RT] = high[at : at + RT - n_low] / jnp.float32(MB * n_dp)
+        out[m, 0:8] = low[m * 8 : (m + 1) * 8] / jnp.float32(MB * n_dp)
+        out[m, 8:16] = high[m * 8 : (m + 1) * 8] / jnp.float32(MB * n_dp)
         rate_out[m, 0:8] = rate
         rate_out[m, 8:16] = rate
 
@@ -357,14 +361,18 @@
             pltpu.VMEM((SLOTS, TOK, LANES), f32),
             pltpu.VMEM((SLOTS, 2, TOK, HID), bf16),
             pltpu.VMEM((SLOTS, TOK, HID), bf16),
-            pltpu.VMEM((BLOCKS, sum(LOW) * YL * C, LANES), bf16),
-            pltpu.VMEM((BLOCKS, sum(LOW) * YL * C, LANES), bf16),
-            pltpu.VMEM((YL * C, (3 * RT - sum(LOW)) * BLOCKS, LANES), bf16),
-            pltpu.VMEM((Y, (3 * RT - sum(LOW)) * BLOCKS, LANES), bf16),
-            pltpu.VMEM((YL * C, sum(LOW), LANES), f32),
-            pltpu.VMEM((Y, sum(LOW), LANES), f32),
-            pltpu.VMEM((BLOCKS, 3 * RT - sum(LOW), LANES), f32),
-            pltpu.VMEM((BLOCKS, 3 * RT - sum(LOW), LANES), f32),
+            pltpu.VMEM((BLOCKS, 2 * LOW * YL * C, LANES), bf16),
+            pltpu.VMEM((BLOCKS, 2 * LOW * YL * C, LANES), bf16),
+            pltpu.VMEM((YL * C, 2 * 8 * BLOCKS, LANES), bf16),
+            pltpu.VMEM((Y, 2 * 8 * BLOCKS, LANES), bf16),
+            pltpu.VMEM((BLOCKS, LOW * YL * C, LANES), bf16),
+            pltpu.VMEM((BLOCKS, LOW * YL * C, LANES), bf16),
+            pltpu.VMEM((YL * C, 8 * BLOCKS, LANES), bf16),
+            pltpu.VMEM((Y, 8 * BLOCKS, LANES), bf16),
+            pltpu.VMEM((YL * C, 3 * LOW, LANES), f32),
+            pltpu.VMEM((Y, 3 * LOW, LANES), f32),
+            pltpu.VMEM((BLOCKS, 24, LANES), f32),
+            pltpu.VMEM((BLOCKS, 24, LANES), f32),
             pltpu.VMEM((4, 8, LANES), f32),
             pltpu.VMEM((BLOCKS, 8, LANES), f32),
             pltpu.VMEM((YH, 8, LANES), f32),
@@ -376,6 +384,8 @@
             dma((SLOTS,)), dma((SLOTS,)),
             dma((SLOTS,)), dma((SLOTS,)),
             dma((SLOTS,)), dma((SLOTS,)),
+            dma((BLOCKS,)), dma((BLOCKS,)),
+            dma((Y,)), dma((Y,)),
             dma((BLOCKS,)), dma((BLOCKS,)),
             dma((Y,)), dma((Y,)),
             dma((Y,)), dma((Y,)),

time: 57.9 us -> 57.7 us (level)
  no operation moved by 1% of the time
where the time goes in v4:
time: 57.7 us; the launch traced here: 57.5 us
  Pallas kernels  54.6 us (95%)
  between operations  1.42 us (2%)
  other arithmetic  1.4 us (2%)
    pallas_call x1, Pallas kernels, per_device(): pl.pallas_call(kernel, out_shape=(jax.ShapeDtypeStruct((3, RT, LANES), f3...  54.6 us
    sub x1, other arithmetic, per_device(): new_master = master - rate * (direction + 0.1 * master)  1.4 us

profile of v4, /device:TPU:1, one launch (start us, length us, event | category | flops | bytes accessed | tf_op | source)
XLA Modules:
  0.0 57.5 jit_solution(5190292661547835775)
XLA Ops:
  1.4 0.0 copy-start
  1.4 0.0 copy-start.1
  1.4 0.0 copy-start.2
  1.4 54.6 %window_grads.1 = (f32[3,16,128]{2,1,0:T(8,128)}, f32[3,16,128]{2,1,0:T(8,128)}) custom-call(bf16[2,16,8192]{2,1,0:T(8,128)(2,1)} %acts_hbm.1, bf16[2,16,8192]{2,1,0:T(8,128)(2,1)} %dy_hbm.1, bf16[16,8192]{1,0:T(8,128)(2,1)} %bitcast.4, bf16[16,8192]{1,0:T(8,128)(2,1)} %bitcast.5, bf16[16,8192]{1,0:T(8,128)(2,1)} %wd_hbm.1, s32[1,2]{1,0:T(1,128)} %ovf_hbm.1), custom_call_target="tpu_custom_call" | custom-call | tf_op jit(solution)/shard_map/window_grads/pallas_call | solution.py:342
  56.0 0.0 copy-done
  56.0 0.0 copy-done.1
  56.0 0.0 copy-done.2
  56.0 1.4 %multiply_subtract_fusion = (f32[3,16,128]{2,1,0:T(8,128)}, f32[3,16,128]{2,1,0:T(8,128)}, f32[3,16,128]{2,1,0:T(8,128)}) fusion(f32[3,16,128]{2,1,0:T(8,128)S(1)} %copy-done, f32[3,16,128]{2,1,0:T(8,128)} %get-tuple-element.5, f32[]{:T(128)} %bitcast.3, f32[]{:T(128)} %bitcast.2, f32[3,16,128]{2,1,0:T(8,128)} %get-tuple-element.6, ...), kind=kLoop, calls=%fused_computation.2 | loop fusion | flops 92160 | bytes 196616 | tf_op jit(solution)/shard_map/sub | solution.py:408
Async XLA Ops:
  1.4 54.7 %copy-start = (f32[3,16,128]{2,1,0:T(8,128)S(1)}, f32[3,16,128]{2,1,0:T(8,128)}, u32[]{:S(2)}) copy-start(f32[3,16,128]{2,1,0:T(8,128)} %param.17) | copy-start | bytes 73732
  1.4 54.7 %copy-start.1 = (f32[3,16,128]{2,1,0:T(8,128)S(1)}, f32[3,16,128]{2,1,0:T(8,128)}, u32[]{:S(2)}) copy-start(f32[3,16,128]{2,1,0:T(8,128)} %param.19) | copy-start | bytes 73732
  1.4 54.7 %copy-start.2 = (f32[3,16,128]{2,1,0:T(8,128)S(1)}, f32[3,16,128]{2,1,0:T(8,128)}, u32[]{:S(2)}) copy-start(f32[3,16,128]{2,1,0:T(8,128)} %param.18) | copy-start | bytes 73732

commit v5 on v4

--- a/solution.py
+++ b/solution.py
@@ -27,7 +27,7 @@
 def kernel(
     acts_hbm, dy_hbm, wg_hbm, wu_hbm, wd_hbm, ovf_hbm, out, rate_out,
     ovf, acts_v, dy_v, w_v, sx, sd, bx, bd, sw, wb, pt, pd, rx, rd, ab, hb, sz, rz, sy, ry, szd, rzd, syd, ryd, s2y, r2y, s2z, r2z,
-    n1, m2, m3, ld, xs, xr, ds, dr, ws, wr, ps, pr, qs, qr, as_, ar, hs, hr, zs, zr, ys, yr, zds, zdr, yds, ydr, y2s, y2r, z2s, z2r,
+    n1, m2, m3, ld, xs, xr, ds, dr, ws, wr, vs, vr, ps, pr, qs, qr, as_, ar, hs, hr, zs, zr, ys, yr, zds, zdr, yds, ydr, y2s, y2r, z2s, z2r,
     n1s, n1r, n2s, n2r, n3s, n3r,
 ):
     dp, t = lax.axis_index("dp"), lax.axis_index("tensor")
@@ -161,12 +161,14 @@
     rows = pl.ds(pl.multiple_of(t * RT, RT), RT)
     half = CC // 2
     one, two = slice(0, half), slice(half, CC)
+    up, down = slice(0, 2), slice(2, 3)
     routes = [(Y - 1, one), (1, two), (Y - 1, two), (1, one)]
     for i, (hop, cols) in enumerate(routes):
         for cp in range(C):
             where = dev(lax.rem(y + hop, Y), z, x, cp)
-            sends.append(send(sw.at[cp, :, :, cols], wb.at[:, rows, cols], ws.at[i * C + cp], wr.at[i * C + c], where))
-    sends.append(send(sw.at[sib], wb.at[:, rows, :], ws.at[8], wr.at[8], dev(y, z, x, sib)))
+            n, to = i * C + cp, i * C + c
+            sends.append(send(sw.at[cp, up, :, cols], wb.at[up, rows, cols], ws.at[n], wr.at[to], where))
+    sends.append(send(sw.at[sib, up], wb.at[up, rows, :], ws.at[8], wr.at[8], dev(y, z, x, sib)))
     for load in loads[3:]:
         load.wait()
     for ex, ez, ec in others:
@@ -188,10 +190,16 @@
 
     for i, (hop, cols) in enumerate(routes[:2]):
         for cp in range(C):
-            arrived(wb.at[:, rows, cols], wr.at[i * C + cp])
+            arrived(wb.at[up, rows, cols], wr.at[i * C + cp])
         shard = pl.ds(pl.multiple_of(lax.rem(yl + YL - hop % YL, YL) * C * RT, C * RT), C * RT)
         where = dev(lax.rem(y + hop, Y), z, x, c)
-        sends.append(send(wb.at[:, shard, cols], wb.at[:, shard, cols], ws.at[9 + i], wr.at[9 + i], where))
+        sends.append(send(wb.at[up, shard, cols], wb.at[up, shard, cols], ws.at[9 + i], wr.at[9 + i], where))
+    hops = [(2, one), (Y - 2, two), (1, slice(0, CC)), (Y - 1, slice(0, CC))]
+    for i, (hop, cols) in enumerate(hops):
+        for cp in range(C):
+            n, to, where = i * C + cp, i * C + c, dev(lax.rem(y + hop, Y), z, x, cp)
+            sends.append(send(sw.at[cp, down, :, cols], wb.at[down, rows, cols], vs.at[n], vr.at[to], where))
+    sends.append(send(sw.at[sib, down], wb.at[down, rows, :], vs.at[8], vr.at[8], dev(y, z, x, sib)))
 
     square = px * 2 + pz
     arrived(m3.at[yh], n3r)
@@ -202,11 +210,11 @@
     pairs = [(1, 1), (1, 0), (0, 1), (0, 0)]
     for i, (hop, cols) in enumerate(routes[2:]):
         for cp in range(C):
-            arrived(wb.at[:, rows, cols], wr.at[(2 + i) * C + cp])
-    arrived(wb.at[:, rows, :], wr.at[8])
+            arrived(wb.at[up, rows, cols], wr.at[(2 + i) * C + cp])
+    arrived(wb.at[up, rows, :], wr.at[8])
     for i, (hop, cols) in enumerate(routes[:2]):
         shard = pl.ds(0, C * RT)
-        arrived(wb.at[:, shard, cols], wr.at[9 + i])
+        arrived(wb.at[up, shard, cols], wr.at[9 + i])
     for ex, ez in pairs:
         for ec in range(C):
             if ex or ez or ec:
@@ -222,6 +230,10 @@
             if ex or ez or ec:
                 n, core = number(ex, ez, ec), across(c, ec)
                 sends.append(send(pt.at[g * C + core], rx.at[me], ps.at[n], pr.at[n], even(ex, ez, core)))
+    for i, (hop, cols) in enumerate(hops):
+        for cp in range(C):
+            arrived(wb.at[down, rows, cols], vr.at[i * C + cp])
+    arrived(wb.at[down, rows, :], vr.at[8])
     for ex, ez in pairs:
         for ec in range(C):
             if ex or ez or ec:
@@ -380,6 +392,7 @@
             dma((SLOTS,)), dma((SLOTS,)),
             dma((SLOTS,)), dma((SLOTS,)),
             dma((11,)), dma((11,)),
+            dma((9,)), dma((9,)),
             dma((SLOTS,)), dma((SLOTS,)),
             dma((SLOTS,)), dma((SLOTS,)),
             dma((SLOTS,)), dma((SLOTS,)),

time: 57.7 us -> 57.4 us (level)
  no operation moved by 1% of the time
where the time goes in v5:
time: 57.4 us; the launch traced here: 57.2 us
  Pallas kernels  54.3 us (95%)
  between operations  1.42 us (2%)
  other arithmetic  1.4 us (2%)
    pallas_call x1, Pallas kernels, per_device(): pl.pallas_call(kernel, out_shape=(jax.ShapeDtypeStruct((3, RT, LANES), f3...  54.3 us
    sub x1, other arithmetic, per_device(): new_master = master - rate * (direction + 0.1 * master)  1.4 us

profile of v5, /device:TPU:1, one launch (start us, length us, event | category | flops | bytes accessed | tf_op | source)
XLA Modules:
  0.0 57.2 jit_solution(815052307537910721)
XLA Ops:
  1.4 0.0 copy-start
  1.4 0.0 copy-start.1
  1.4 0.0 copy-start.2
  1.4 54.3 %window_grads.1 = (f32[3,16,128]{2,1,0:T(8,128)}, f32[3,16,128]{2,1,0:T(8,128)}) custom-call(bf16[2,16,8192]{2,1,0:T(8,128)(2,1)} %acts_hbm.1, bf16[2,16,8192]{2,1,0:T(8,128)(2,1)} %dy_hbm.1, bf16[16,8192]{1,0:T(8,128)(2,1)} %bitcast.4, bf16[16,8192]{1,0:T(8,128)(2,1)} %bitcast.5, bf16[16,8192]{1,0:T(8,128)(2,1)} %wd_hbm.1, s32[1,2]{1,0:T(1,128)} %ovf_hbm.1), custom_call_target="tpu_custom_call" | custom-call | tf_op jit(solution)/shard_map/window_grads/pallas_call | solution.py:354
  55.7 0.0 copy-done
  55.8 0.0 copy-done.1
  55.8 0.0 copy-done.2
  55.8 1.4 %multiply_subtract_fusion = (f32[3,16,128]{2,1,0:T(8,128)}, f32[3,16,128]{2,1,0:T(8,128)}, f32[3,16,128]{2,1,0:T(8,128)}) fusion(f32[3,16,128]{2,1,0:T(8,128)S(1)} %copy-done, f32[3,16,128]{2,1,0:T(8,128)} %get-tuple-element.5, f32[]{:T(128)} %bitcast.3, f32[]{:T(128)} %bitcast.2, f32[3,16,128]{2,1,0:T(8,128)} %get-tuple-element.6, ...), kind=kLoop, calls=%fused_computation.2 | loop fusion | flops 92160 | bytes 196616 | tf_op jit(solution)/shard_map/sub | solution.py:421
Async XLA Ops:
  1.4 54.4 %copy-start = (f32[3,16,128]{2,1,0:T(8,128)S(1)}, f32[3,16,128]{2,1,0:T(8,128)}, u32[]{:S(2)}) copy-start(f32[3,16,128]{2,1,0:T(8,128)} %param.17) | copy-start | bytes 73732
  1.4 54.4 %copy-start.1 = (f32[3,16,128]{2,1,0:T(8,128)S(1)}, f32[3,16,128]{2,1,0:T(8,128)}, u32[]{:S(2)}) copy-start(f32[3,16,128]{2,1,0:T(8,128)} %param.19) | copy-start | bytes 73732
  1.4 54.4 %copy-start.2 = (f32[3,16,128]{2,1,0:T(8,128)S(1)}, f32[3,16,128]{2,1,0:T(8,128)}, u32[]{:S(2)}) copy-start(f32[3,16,128]{2,1,0:T(8,128)} %param.18) | copy-start | bytes 73732

commit v6 on v5

--- a/solution.py
+++ b/solution.py
@@ -313,17 +313,19 @@
         k = lax.rem(kme + rel, BLOCKS)
         sends.append(send(m2.at[kme], m2.at[kme], n2s.at[rel], n2r.at[kme], class_dev(k)))
     from_y(syd, ryd, yds, ydr)
+    high_down = added(ryd, Y)
+    from_z(rzd, zdr)
+    low_down = added(rzd, BLOCKS)
     from_y(sy, ry, ys, yr)
-    high = (added(ry, Y), added(ryd, Y))
+    high = (added(ry, Y), high_down)
     for k in range(BLOCKS):
         for m in range(3):
             at = m % 2 * 8 * BLOCKS + k * 8
             s2z[k, m * 8 : (m + 1) * 8] = high[m // 2][at : at + 8]
     to_z(s2z, r2z, z2s, z2r, near + far)
     r2z[kme] = s2z[kme]
-    from_z(rzd, zdr)
     from_z(rz, zr)
-    low = (added(rz, BLOCKS), added(rzd, BLOCKS))
+    low = (added(rz, BLOCKS), low_down)
     for i in range(YL * C):
         for m in range(3):
             at = m % 2 * LOW * YL * C + i * LOW

time: 57.4 us -> 57.4 us (level)
  no operation moved by 1% of the time
where the time goes in v6:
time: 57.4 us; the launch traced here: 57.1 us
  Pallas kernels  54.3 us (95%)
  between operations  1.42 us (2%)
  other arithmetic  1.4 us (2%)
    pallas_call x1, Pallas kernels, per_device(): pl.pallas_call(kernel, out_shape=(jax.ShapeDtypeStruct((3, RT, LANES), f3...  54.3 us
    sub x1, other arithmetic, per_device(): new_master = master - rate * (direction + 0.1 * master)  1.4 us

profile of v6, /device:TPU:1, one launch (start us, length us, event | category | flops | bytes accessed | tf_op | source)
XLA Modules:
  0.0 57.1 jit_solution(9797244370545593216)
XLA Ops:
  1.4 0.0 copy-start
  1.4 0.0 copy-start.1
  1.4 0.0 copy-start.2
  1.4 54.3 %window_grads.1 = (f32[3,16,128]{2,1,0:T(8,128)}, f32[3,16,128]{2,1,0:T(8,128)}) custom-call(bf16[2,16,8192]{2,1,0:T(8,128)(2,1)} %acts_hbm.1, bf16[2,16,8192]{2,1,0:T(8,128)(2,1)} %dy_hbm.1, bf16[16,8192]{1,0:T(8,128)(2,1)} %bitcast.4, bf16[16,8192]{1,0:T(8,128)(2,1)} %bitcast.5, bf16[16,8192]{1,0:T(8,128)(2,1)} %wd_hbm.1, s32[1,2]{1,0:T(1,128)} %ovf_hbm.1), custom_call_target="tpu_custom_call" | custom-call | tf_op jit(solution)/shard_map/window_grads/pallas_call | solution.py:356
  55.7 0.0 copy-done
  55.7 0.0 copy-done.1
  55.7 0.0 copy-done.2
  55.7 1.4 %multiply_subtract_fusion = (f32[3,16,128]{2,1,0:T(8,128)}, f32[3,16,128]{2,1,0:T(8,128)}, f32[3,16,128]{2,1,0:T(8,128)}) fusion(f32[3,16,128]{2,1,0:T(8,128)S(1)} %copy-done, f32[3,16,128]{2,1,0:T(8,128)} %get-tuple-element.5, f32[]{:T(128)} %bitcast.3, f32[]{:T(128)} %bitcast.2, f32[3,16,128]{2,1,0:T(8,128)} %get-tuple-element.6, ...), kind=kLoop, calls=%fused_computation.2 | loop fusion | flops 92160 | bytes 196616 | tf_op jit(solution)/shard_map/sub | solution.py:423
Async XLA Ops:
  1.4 54.3 %copy-start = (f32[3,16,128]{2,1,0:T(8,128)S(1)}, f32[3,16,128]{2,1,0:T(8,128)}, u32[]{:S(2)}) copy-start(f32[3,16,128]{2,1,0:T(8,128)} %param.17) | copy-start | bytes 73732
  1.4 54.3 %copy-start.1 = (f32[3,16,128]{2,1,0:T(8,128)S(1)}, f32[3,16,128]{2,1,0:T(8,128)}, u32[]{:S(2)}) copy-start(f32[3,16,128]{2,1,0:T(8,128)} %param.19) | copy-start | bytes 73732
  1.4 54.3 %copy-start.2 = (f32[3,16,128]{2,1,0:T(8,128)S(1)}, f32[3,16,128]{2,1,0:T(8,128)}, u32[]{:S(2)}) copy-start(f32[3,16,128]{2,1,0:T(8,128)} %param.18) | copy-start | bytes 73732
